TPU v7x, 32 devices: a whole 2x2x4 slice. The times are simulated.
32 devices in a mesh: dp: 16 (over z, x, core), tensor: 2 (over y).
Axes of the slice: x: 2, y: 2, z: 4, core: 2. Of those that a mesh axis runs over, the one named last changes fastest.
Arguments:
- tokens: bfloat16 [32, 256, 1024], P('dp', 'tensor'), may hold values from -6 to 6
- encoder: bfloat16 [32, 128, 1024], P('dp', 'tensor'), may hold values from -6 to 6
- target_doc: int32 [32, 256], P('dp'), may hold values from 0 to 1, as said below
- source_doc: int32 [32, 128], P('dp'), may hold values from 0 to 1, as said below
- self_proj: bfloat16 [1024, 3, 1024], P('dp', None, 'tensor'), may hold values from -0.1875 to 0.1875
- self_out: bfloat16 [1024, 1024], P('tensor', 'dp'), may hold values from -1 to 1
- cross_query: bfloat16 [1024, 1024], P('dp', 'tensor'), may hold values from -0.1875 to 0.1875
- cross_pairs: bfloat16 [1024, 2, 1024], P('dp', None, 'tensor'), may hold values from -0.1875 to 0.1875
- cross_out: bfloat16 [1024, 1024], P('tensor', 'dp'), may hold values from -1 to 1
- hidden_in: bfloat16 [1024, 8192], P(None, ('dp', 'tensor')), may hold values from -0.1875 to 0.1875
- hidden_in_bias: bfloat16 [8192], P(('dp', 'tensor')), may hold values from -3 to 3
- hidden_out: bfloat16 [8192, 1024], P(('dp', 'tensor')), may hold values from -0.09375 to 0.09375
- hidden_out_bias: float32 [1024], P(('dp', 'tensor')), may hold values from -5 to 5
- self_gain: float32 [1024], P(('dp', 'tensor')), may hold values from 0.5 to 1.5
- self_shift: float32 [1024], P(('dp', 'tensor')), may hold values from -1.75 to 1.75
- cross_gain: float32 [1024], P(('dp', 'tensor')), may hold values from 0.5 to 1.5
- cross_shift: float32 [1024], P(('dp', 'tensor')), may hold values from -1.75 to 1.75
- hidden_gain: float32 [1024], P(('dp', 'tensor')), may hold values from 0.5 to 1.5
- hidden_shift: float32 [1024], P(('dp', 'tensor')), may hold values from -1.75 to 1.75
- cotangent: bfloat16 [32, 256, 1024], P('dp', 'tensor'), may hold values from -8 to 8
Outputs:
- result: float32 [32, 256, 1024], P('dp', 'tensor')
- token_grad: float32 [32, 256, 1024], P('dp', 'tensor')
- encoder_grad: float32 [32, 128, 1024], P('dp', 'tensor')
- grad_self_proj: float32 [1024, 3, 1024], P('dp', None, 'tensor')
- grad_self_out: float32 [1024, 1024], P('tensor', 'dp')
- grad_cross_query: float32 [1024, 1024], P('dp', 'tensor')
- grad_cross_pairs: float32 [1024, 2, 1024], P('dp', None, 'tensor')
- grad_cross_out: float32 [1024, 1024], P('tensor', 'dp')
- grad_hidden_in: float32 [1024, 8192], P(None, ('dp', 'tensor'))
- grad_hidden_in_bias: float32 [8192], P(('dp', 'tensor'))
- grad_hidden_out: float32 [8192, 1024], P(('dp', 'tensor'))
- grad_hidden_out_bias: float32 [1024], P(('dp', 'tensor'))
- grad_self_gain: float32 [1024], P(('dp', 'tensor'))
- grad_self_shift: float32 [1024], P(('dp', 'tensor'))
- grad_cross_gain: float32 [1024], P(('dp', 'tensor'))
- grad_cross_shift: float32 [1024], P(('dp', 'tensor'))
- grad_hidden_gain: float32 [1024], P(('dp', 'tensor'))
- grad_hidden_shift: float32 [1024], P(('dp', 'tensor'))
Inputs may be any that keep to these rules, and one draw needn't show every extreme that they name: `target_doc`: in each row the numbers are 0 on a first run of 64 to 256 positions, the target sequence, and 1 on the padding after it; some row has no padding. `source_doc`: in each row the numbers are 0 on a first run of 32 to 96 positions, the source sentence, and 1 on the padding after it; some row has a run of exactly 32.
All inputs are finite; a program needn't handle non-finite values.
Results may differ from a plain program's by a relative error of at most 0.024.
Values may be sent and summed in bfloat16 or wider, within the bound.
A program may use at most 120 MiB of HBM per device.

v0:
```python
import jax
import jax.numpy as jnp
from jax import lax
from jax.sharding import PartitionSpec as P

HEAD = 64


EPS = 1e-05
NEGATIVE = -1e30
BLOCK_ROWS = 512


def smooth_gate(values):
    return jax.nn.gelu(values, approximate=True)


def norm_forward(hidden, norm_gain, norm_shift):
    center = hidden - jnp.mean(hidden, axis=-1, keepdims=True)
    inverse = lax.rsqrt(jnp.mean(center * center, axis=-1, keepdims=True) + EPS)
    normal = center * inverse
    return (normal * norm_gain + norm_shift, normal, inverse)


def norm_backward(upward, normal, inverse, norm_gain):
    scaled = upward * norm_gain
    centred = (
        scaled
        - jnp.mean(scaled, axis=-1, keepdims=True)
        - normal * jnp.mean(scaled * normal, axis=-1, keepdims=True)
    )
    return (centred * inverse, jnp.sum(upward * normal, axis=0), jnp.sum(upward, axis=0))


def split_blocks(array):
    row_count = array.shape[0]
    block_size = min(BLOCK_ROWS, row_count)
    return array.reshape((row_count // block_size, block_size) + array.shape[1:])


def block_scores(query_block, key_rows, allow_block):
    query_heads = query_block.reshape(query_block.shape[0], -1, HEAD)
    key_heads = key_rows.reshape(key_rows.shape[0], -1, HEAD)
    scores = jnp.einsum(
        "qhd,khd->hqk", query_heads, key_heads, preferred_element_type=jnp.float32
    ) * HEAD ** (-0.5)
    return jnp.where(allow_block[None], scores, NEGATIVE)


def attend(queries, key_rows, values, allowed):
    columns = queries.shape[1]
    value_heads = values.reshape(values.shape[0], -1, HEAD)

    def one_block(pieces):
        query_block, allow_block = pieces
        scores = block_scores(query_block, key_rows, allow_block)
        highest = jnp.max(scores, axis=-1, keepdims=True)
        exponent = jnp.exp(scores - highest)
        totals = jnp.sum(exponent, axis=-1, keepdims=True)
        softmaxed = (exponent / totals).astype(jnp.bfloat16)
        mixture = jnp.einsum(
            "hqk,khd->qhd", softmaxed, value_heads, preferred_element_type=jnp.float32
        )
        return (
            mixture.reshape(query_block.shape[0], columns).astype(jnp.bfloat16),
            (highest + jnp.log(totals))[..., 0],
        )

    mixture, logsum = lax.map(one_block, (split_blocks(queries), split_blocks(allowed)))
    return (mixture.reshape(queries.shape), logsum)


def attend_backward(queries, key_rows, values, allowed, logsum, slope_heads):
    scaling = HEAD ** (-0.5)
    key_heads = key_rows.reshape(key_rows.shape[0], -1, HEAD)
    value_heads = values.reshape(values.shape[0], -1, HEAD)

    def one_block(running, pieces):
        key_total, value_total = running
        query_block, allow_block, logsum_block, slope_block = pieces
        scores = block_scores(query_block, key_rows, allow_block)
        softmaxed = jnp.exp(scores - logsum_block[..., None])
        query_heads = query_block.reshape(query_block.shape[0], -1, HEAD)
        slope_out = slope_block.reshape(slope_block.shape[0], -1, HEAD)
        slope_probs = jnp.einsum(
            "qhd,khd->hqk", slope_out, value_heads, preferred_element_type=jnp.float32
        )
        centred = jnp.sum(softmaxed * slope_probs, axis=-1, keepdims=True)
        slope_scores = (softmaxed * (slope_probs - centred)).astype(jnp.bfloat16)
        slope_query = (
            jnp.einsum("hqk,khd->qhd", slope_scores, key_heads, preferred_element_type=jnp.float32)
            * scaling
        )
        key_total = (
            key_total
            + jnp.einsum(
                "hqk,qhd->khd", slope_scores, query_heads, preferred_element_type=jnp.float32
            )
            * scaling
        )
        value_total = value_total + jnp.einsum(
            "hqk,qhd->khd",
            softmaxed.astype(jnp.bfloat16),
            slope_out,
            preferred_element_type=jnp.float32,
        )
        return (
            (key_total, value_total),
            slope_query.reshape(query_block.shape[0], -1).astype(jnp.bfloat16),
        )

    empty_heads = jnp.zeros(key_heads.shape, jnp.float32)
    (key_total, value_total), slope_query = lax.scan(
        one_block,
        (empty_heads, empty_heads),
        (split_blocks(queries), split_blocks(allowed), logsum, split_blocks(slope_heads)),
    )
    return (
        slope_query.reshape(queries.shape),
        key_total.reshape(key_rows.shape).astype(jnp.bfloat16),
        value_total.reshape(values.shape).astype(jnp.bfloat16),
    )


def gather_rows(local_rows):
    return lax.all_gather(local_rows, "tensor", axis=0, tiled=True)


def sum_rows(partial_sum):
    return lax.psum_scatter(
        partial_sum.astype(jnp.bfloat16), "tensor", scatter_dimension=0, tiled=True
    ).astype(jnp.float32)


def gather_slopes(local_slopes):
    return lax.all_gather(local_slopes, "tensor", axis=0, tiled=True)


def sum_slopes(partial_sum):
    return lax.psum_scatter(
        partial_sum.astype(jnp.bfloat16), "tensor", scatter_dimension=0, tiled=True
    ).astype(jnp.float32)


def reduce_weights(weight_terms):
    return (
        lax.psum_scatter(weight_terms[0], "dp", scatter_dimension=0, tiled=True),
        lax.psum_scatter(weight_terms[1], "dp", scatter_dimension=1, tiled=True),
        lax.psum_scatter(weight_terms[2], "dp", scatter_dimension=0, tiled=True),
        lax.psum_scatter(weight_terms[3], "dp", scatter_dimension=0, tiled=True),
        lax.psum_scatter(weight_terms[4], "dp", scatter_dimension=1, tiled=True),
        lax.psum_scatter(weight_terms[5], "dp", scatter_dimension=1, tiled=True),
        lax.psum_scatter(weight_terms[6], "dp", scatter_dimension=0, tiled=True),
        lax.psum_scatter(weight_terms[7], "dp", scatter_dimension=0, tiled=True),
    )


def local(
    tokens,
    encoder,
    target_doc,
    source_doc,
    self_proj,
    self_out,
    cross_query,
    cross_pairs,
    cross_out,
    hidden_in,
    hidden_in_bias,
    hidden_out,
    hidden_out_bias,
    self_gain,
    self_shift,
    cross_gain,
    cross_shift,
    hidden_gain,
    hidden_shift,
    cotangent,
):
    (
        full_self_gain,
        full_self_shift,
        full_cross_gain,
        full_cross_shift,
        full_hidden_gain,
        full_hidden_shift,
        full_out_bias,
    ) = (
        lax.all_gather(self_gain, ("dp", "tensor"), axis=0, tiled=True),
        lax.all_gather(self_shift, ("dp", "tensor"), axis=0, tiled=True),
        lax.all_gather(cross_gain, ("dp", "tensor"), axis=0, tiled=True),
        lax.all_gather(cross_shift, ("dp", "tensor"), axis=0, tiled=True),
        lax.all_gather(hidden_gain, ("dp", "tensor"), axis=0, tiled=True),
        lax.all_gather(hidden_shift, ("dp", "tensor"), axis=0, tiled=True),
        lax.all_gather(hidden_out_bias, ("dp", "tensor"), axis=0, tiled=True),
    )
    micro_count = tokens.shape[0]
    row_count = tokens.shape[1] * lax.axis_size("tensor")
    positions = jnp.arange(row_count)
    results = []
    token_grads = []
    encoder_grads = []
    vector_total = None
    weight_total = None
    for step_index in range(micro_count):
        forward_weights = (
            lax.all_gather(self_proj, "dp", axis=0, tiled=True),
            lax.all_gather(self_out, "dp", axis=1, tiled=True),
            lax.all_gather(cross_query, "dp", axis=0, tiled=True),
            lax.all_gather(cross_pairs, "dp", axis=0, tiled=True),
            lax.all_gather(cross_out, "dp", axis=1, tiled=True),
            lax.all_gather(hidden_in, "dp", axis=1, tiled=True),
            lax.all_gather(hidden_in_bias, "dp", axis=0, tiled=True),
            lax.all_gather(hidden_out, "dp", axis=0, tiled=True),
        )
        (
            full_proj,
            full_self_out,
            full_query,
            full_pairs,
            full_cross_out,
            full_in,
            full_in_bias,
            full_out,
        ) = forward_weights
        target_row = target_doc[step_index]
        source_row = source_doc[step_index]
        self_allowed = (target_row[:, None] == target_row[None, :]) & (
            positions[None, :] <= positions[:, None]
        )
        cross_allowed = target_row[:, None] == source_row[None, :]
        start_hidden = tokens[step_index].astype(jnp.float32)
        normed_first, normal_first, inverse_first = norm_forward(
            start_hidden, full_self_gain, full_self_shift
        )
        self_rows = gather_rows(normed_first.astype(jnp.bfloat16))
        triple = jnp.einsum(
            "td,dcj->tcj", self_rows, full_proj, preferred_element_type=jnp.float32
        ).astype(jnp.bfloat16)
        self_heads, self_logsum = attend(triple[:, 0], triple[:, 1], triple[:, 2], self_allowed)
        middle = start_hidden + sum_rows(
            jnp.dot(self_heads, full_self_out, preferred_element_type=jnp.float32)
        )
        normed_second, normal_second, inverse_second = norm_forward(
            middle, full_cross_gain, full_cross_shift
        )
        cross_rows, source_rows = (
            lax.all_gather(normed_second.astype(jnp.bfloat16), "tensor", axis=0, tiled=True),
            lax.all_gather(encoder[step_index], "tensor", axis=0, tiled=True),
        )
        cross_queries = jnp.dot(cross_rows, full_query, preferred_element_type=jnp.float32).astype(
            jnp.bfloat16
        )
        key_value = jnp.einsum(
            "sd,dcj->scj", source_rows, full_pairs, preferred_element_type=jnp.float32
        ).astype(jnp.bfloat16)
        cross_heads, cross_logsum = attend(
            cross_queries, key_value[:, 0], key_value[:, 1], cross_allowed
        )
        latter = middle + sum_rows(
            jnp.dot(cross_heads, full_cross_out, preferred_element_type=jnp.float32)
        )
        normed_third, normal_third, inverse_third = norm_forward(
            latter, full_hidden_gain, full_hidden_shift
        )
        hidden_rows = gather_rows(normed_third.astype(jnp.bfloat16))
        before = jnp.dot(
            hidden_rows, full_in, preferred_element_type=jnp.float32
        ) + full_in_bias.astype(jnp.float32)
        gated, gate_pullback = jax.vjp(smooth_gate, before)
        active = gated.astype(jnp.bfloat16)
        results.append(
            latter
            + sum_rows(jnp.dot(active, full_out, preferred_element_type=jnp.float32))
            + full_out_bias
        )
        back_weights = (
            lax.all_gather(self_proj, "dp", axis=0, tiled=True),
            lax.all_gather(self_out, "dp", axis=1, tiled=True),
            lax.all_gather(cross_query, "dp", axis=0, tiled=True),
            lax.all_gather(cross_pairs, "dp", axis=0, tiled=True),
            lax.all_gather(cross_out, "dp", axis=1, tiled=True),
            lax.all_gather(hidden_in, "dp", axis=1, tiled=True),
            lax.all_gather(hidden_in_bias, "dp", axis=0, tiled=True),
            lax.all_gather(hidden_out, "dp", axis=0, tiled=True),
        )
        (
            back_proj,
            back_self_out,
            back_query,
            back_pairs,
            back_cross_out,
            back_in,
            back_in_bias,
            back_out,
        ) = back_weights
        upward = cotangent[step_index].astype(jnp.float32)
        grad_out_bias = jnp.sum(upward, axis=0)
        slope_rows = gather_slopes(upward.astype(jnp.bfloat16))
        grad_out = jnp.einsum("tf,td->fd", active, slope_rows, preferred_element_type=jnp.float32)
        slope_active = jnp.einsum(
            "td,fd->tf", slope_rows, back_out, preferred_element_type=jnp.float32
        )
        slope_before = gate_pullback(slope_active)[0].astype(jnp.bfloat16)
        grad_in_bias = jnp.sum(slope_before.astype(jnp.float32), axis=0)
        grad_in = jnp.einsum(
            "td,tf->df", hidden_rows, slope_before, preferred_element_type=jnp.float32
        )
        slope_normed = sum_slopes(
            jnp.einsum("tf,df->td", slope_before, back_in, preferred_element_type=jnp.float32)
        )
        slope_hidden, grad_hidden_gain, grad_hidden_shift = norm_backward(
            slope_normed, normal_third, inverse_third, full_hidden_gain
        )
        upward = upward + slope_hidden
        slope_rows = gather_slopes(upward.astype(jnp.bfloat16))
        grad_cross_out = jnp.einsum(
            "tj,td->jd", cross_heads, slope_rows, preferred_element_type=jnp.float32
        )
        slope_heads = jnp.einsum(
            "td,jd->tj", slope_rows, back_cross_out, preferred_element_type=jnp.float32
        ).astype(jnp.bfloat16)
        slope_query, slope_keys, slope_values = attend_backward(
            cross_queries,
            key_value[:, 0],
            key_value[:, 1],
            cross_allowed,
            cross_logsum,
            slope_heads,
        )
        slope_pairs = jnp.stack([slope_keys, slope_values], axis=1)
        grad_query = jnp.einsum(
            "td,tj->dj", cross_rows, slope_query, preferred_element_type=jnp.float32
        )
        grad_pairs = jnp.einsum(
            "sd,scj->dcj", source_rows, slope_pairs, preferred_element_type=jnp.float32
        )
        slope_cross, slope_source = (
            lax.psum_scatter(
                jnp.einsum(
                    "tj,dj->td", slope_query, back_query, preferred_element_type=jnp.float32
                ).astype(jnp.bfloat16),
                "tensor",
                scatter_dimension=0,
                tiled=True,
            ).astype(jnp.float32),
            lax.psum_scatter(
                jnp.einsum(
                    "scj,dcj->sd", slope_pairs, back_pairs, preferred_element_type=jnp.float32
                ).astype(jnp.bfloat16),
                "tensor",
                scatter_dimension=0,
                tiled=True,
            ).astype(jnp.float32),
        )
        slope_hidden, grad_cross_gain, grad_cross_shift = norm_backward(
            slope_cross, normal_second, inverse_second, full_cross_gain
        )
        upward = upward + slope_hidden
        slope_rows = gather_slopes(upward.astype(jnp.bfloat16))
        grad_self_out = jnp.einsum(
            "tj,td->jd", self_heads, slope_rows, preferred_element_type=jnp.float32
        )
        slope_heads = jnp.einsum(
            "td,jd->tj", slope_rows, back_self_out, preferred_element_type=jnp.float32
        ).astype(jnp.bfloat16)
        slope_query, slope_keys, slope_values = attend_backward(
            triple[:, 0], triple[:, 1], triple[:, 2], self_allowed, self_logsum, slope_heads
        )
        slope_triple = jnp.stack([slope_query, slope_keys, slope_values], axis=1)
        grad_proj = jnp.einsum(
            "td,tcj->dcj", self_rows, slope_triple, preferred_element_type=jnp.float32
        )
        slope_self = sum_slopes(
            jnp.einsum("tcj,dcj->td", slope_triple, back_proj, preferred_element_type=jnp.float32)
        )
        slope_hidden, grad_self_gain, grad_self_shift = norm_backward(
            slope_self, normal_first, inverse_first, full_self_gain
        )
        token_grads.append(upward + slope_hidden)
        encoder_grads.append(slope_source)
        vector_terms = (
            grad_self_gain,
            grad_self_shift,
            grad_cross_gain,
            grad_cross_shift,
            grad_hidden_gain,
            grad_hidden_shift,
            grad_out_bias,
        )
        vector_total = (
            vector_terms if step_index == 0 else jax.tree.map(jnp.add, vector_total, vector_terms)
        )
        weight_terms = (
            grad_proj,
            grad_self_out,
            grad_query,
            grad_pairs,
            grad_cross_out,
            grad_in,
            grad_in_bias,
            grad_out,
        )
        shard_terms = reduce_weights(weight_terms)
        weight_total = (
            shard_terms if step_index == 0 else jax.tree.map(jnp.add, weight_total, shard_terms)
        )
    vector_shards = (
        lax.psum_scatter(vector_total[0], ("dp", "tensor"), scatter_dimension=0, tiled=True),
        lax.psum_scatter(vector_total[1], ("dp", "tensor"), scatter_dimension=0, tiled=True),
        lax.psum_scatter(vector_total[2], ("dp", "tensor"), scatter_dimension=0, tiled=True),
        lax.psum_scatter(vector_total[3], ("dp", "tensor"), scatter_dimension=0, tiled=True),
        lax.psum_scatter(vector_total[4], ("dp", "tensor"), scatter_dimension=0, tiled=True),
        lax.psum_scatter(vector_total[5], ("dp", "tensor"), scatter_dimension=0, tiled=True),
        lax.psum_scatter(vector_total[6], ("dp", "tensor"), scatter_dimension=0, tiled=True),
    )
    return (
        jnp.stack(results),
        jnp.stack(token_grads),
        jnp.stack(encoder_grads),
        weight_total[0],
        weight_total[1],
        weight_total[2],
        weight_total[3],
        weight_total[4],
        weight_total[5],
        weight_total[6],
        weight_total[7],
        vector_shards[6],
        vector_shards[0],
        vector_shards[1],
        vector_shards[2],
        vector_shards[3],
        vector_shards[4],
        vector_shards[5],
    )


def solution(mesh):
    in_specs = (
        P("dp", "tensor", None),
        P("dp", "tensor", None),
        P("dp", None),
        P("dp", None),
        P("dp", None, "tensor"),
        P("tensor", "dp"),
        P("dp", "tensor"),
        P("dp", None, "tensor"),
        P("tensor", "dp"),
        P(None, ("dp", "tensor")),
        P(("dp", "tensor")),
        P(("dp", "tensor"), None),
        P(("dp", "tensor")),
        P(("dp", "tensor")),
        P(("dp", "tensor")),
        P(("dp", "tensor")),
        P(("dp", "tensor")),
        P(("dp", "tensor")),
        P(("dp", "tensor")),
        P("dp", "tensor", None),
    )
    out_specs = (
        P("dp", "tensor", None),
        P("dp", "tensor", None),
        P("dp", "tensor", None),
        P("dp", None, "tensor"),
        P("tensor", "dp"),
        P("dp", "tensor"),
        P("dp", None, "tensor"),
        P("tensor", "dp"),
        P(None, ("dp", "tensor")),
        P(("dp", "tensor")),
        P(("dp", "tensor"), None),
        P(("dp", "tensor")),
        P(("dp", "tensor")),
        P(("dp", "tensor")),
        P(("dp", "tensor")),
        P(("dp", "tensor")),
        P(("dp", "tensor")),
        P(("dp", "tensor")),
    )
    return jax.shard_map(local, mesh=mesh, in_specs=in_specs, out_specs=out_specs, check_vma=False)
```

profile of v0, /device:TPU:0, one launch (start us, length us, event | category | flops | bytes accessed | tf_op | source)
XLA Modules:
  0.0 1425.6 jit_solution(5765985157803851402)
XLA Ops:
  16.1 42.9 %all-reduce.17 = (f32[1024]{0:T(1024)}, f32[1024]{0:T(1024)S(1)}, f32[1024]{0:T(1024)S(1)}, f32[1024]{0:T(1024)S(1)}, f32[1024]{0:T(1024)}, /*index=5*/f32[1024]{0:T(1024)S(1)}) all-reduce(f32[1024]{0:T(1024)S(1)} %dynamic-update-slice.3, f32[1024]{0:T(1024)S(1)} %dynamic-update-slice.2, ...), channel_id=1, replica_groups=mesh['dp'=16,'tensor'=2] {'dp','tensor'}, use_global_device_ids=true, to_apply=%add.3 | all-reduce | flops 6144 | bytes 49152
  60.2 8.3 all_gather.111
  69.4 2.9 convolution_convert_fusion.1
  74.3 23.1 %all-gather.15.cloned.1.call-done = bf16[512,1024]{0,1:T(8,128)(2,1)} async-done(((bf16[512,64]{0,1:T(8,128)(2,1)}), bf16[512,1024]{0,1:T(8,128)(2,1)}) %all-gather.15.cloned.1.call-update) | async-done | bytes 1048592 | tf_op jit(solution)/shard_map/all_gather | solution.py:208
  97.4 2.5 convolution_convert_fusion.11
  100.9 12.9 reduce-scatter.21.cloned.1.call-done
  115.7 8.7 all_gather.128
  124.4 3.1 convolution_convert_fusion
  136.1 5.8 all-gather
  141.9 5.6 all-gather.1
  148.3 9.7 all-gather.17.cloned.1.call-done
  170.7 3.4 reduce-scatter.27.cloned.1.call-done
  178.5 8.7 all_gather.130
  187.2 26.9 %all-gather.19.cloned.1.call-done = bf16[1024,512]{1,0:T(8,128)(2,1)} async-done(((bf16[64,512]{1,0:T(8,128)(2,1)}), bf16[1024,512]{1,0:T(8,128)(2,1)}) %all-gather.19.cloned.1.call-update) | async-done | bytes 1048592 | tf_op jit(solution)/shard_map/all_gather | solution.py:209
  214.1 2.4 convolution_convert_fusion.19
  218.2 11.0 all_gather.118
  233.5 19.7 %all-gather.21.cloned.1.call-done = bf16[512,1024]{0,1:T(8,128)(2,1)} async-done(((bf16[512,64]{0,1:T(8,128)(2,1)}), bf16[512,1024]{0,1:T(8,128)(2,1)}) %all-gather.21.cloned.1.call-update) | async-done | bytes 1048592 | tf_op jit(solution)/shard_map/all_gather | solution.py:211
  253.2 2.6 convolution_convert_fusion.7
  255.9 2.5 convolution_convert_fusion.23
  266.2 19.3 %all-gather.4 = bf16[16,1,256]{2,1,0:T(2,128)(2,1)S(1)} all-gather(bf16[1,1,256]{2,1,0:T(2,128)(2,1)S(1)} %reshape.504), channel_id=1, replica_groups=mesh['dp'=16,'tensor'=2] {'dp'}, dimensions={0}, use_global_device_ids=true | all-gather | bytes 8704 | tf_op jit(solution)/shard_map/all_gather | solution.py:213
  286.1 9.3 all-gather.3
  295.5 8.5 all-gather.2
  306.4 7.6 all_gather.123
  314.0 7.2 all_gather.131
  321.2 47.6 %all-gather.23.cloned.1.call-done = bf16[1024,4096]{1,0:T(8,128)(2,1)} async-done(((bf16[1024,256]{1,0:T(8,128)(2,1)}), bf16[1024,4096]{1,0:T(8,128)(2,1)}) %all-gather.23.cloned.1.call-update) | async-done | bytes 8388624 | tf_op jit(solution)/shard_map/all_gather | solution.py:212
  368.7 7.8 convolution_add_fusion.2
  376.5 67.5 %all-gather.25.cloned.1.call-done = bf16[4096,1024]{1,0:T(8,128)(2,1)} async-done(((bf16[256,1024]{1,0:T(8,128)(2,1)}), bf16[4096,1024]{1,0:T(8,128)(2,1)}) %all-gather.25.cloned.1.call-update) | async-done | bytes 8388624 | tf_op jit(solution)/shard_map/all_gather | solution.py:214
  444.0 8.5 convert_reduce_fusion
  453.8 3.2 convolution_convert_fusion.3
  457.5 5.9 convolution_add_fusion.3
  463.8 5.6 convert_reduce_fusion.1
  470.8 3.2 convolution_convert_fusion.5
  478.1 9.4 reduce-scatter.33.cloned.1.call-done
  487.5 2.5 fusion.105
  490.0 2.9 fusion.149
  492.8 8.7 all_gather.136
  505.3 8.0 all_gather.133
  514.1 2.4 convolution_convert_fusion.17
  542.1 3.3 fusion.22
  549.2 3.2 fusion.23
  554.4 2.7 add_bitcast_fusion
  557.1 7.3 copy.197
  567.0 2.9 fusion.145
  569.9 7.0 all_gather.137
  580.0 8.5 all_gather.134
  589.3 2.4 convolution_convert_fusion.16
  601.6 2.6 fusion.25
  606.0 4.0 fusion.20
  619.1 3.9 fusion.21
  623.3 8.3 convolution_convert_fusion.6
  631.6 8.3 convolution_convert_fusion.9
  651.5 3.7 convolution_add_fusion.4
  656.2 10.9 fusion.115
  667.1 11.6 convolution_add_fusion
  679.7 4.0 fusion.169
  683.7 9.8 convolution_add_fusion.1
  696.5 59.5 %all-reduce.8 = f32[4096]{0:T(1024)S(1)} all-reduce(f32[4096]{0:T(1024)S(1)} %add.421), channel_id=34, replica_groups=mesh['dp'=16,'tensor'=2] {'dp'}, use_global_device_ids=true, to_apply=%region_63.64.clone | all-reduce | flops 4096 | bytes 32768
  762.0 37.4 %all-reduce.16 = (f32[1024]{0:T(1024)S(1)}, f32[1024]{0:T(1024)S(1)}, f32[1024]{0:T(1024)S(1)}, f32[1024]{0:T(1024)S(1)}, f32[1024]{0:T(1024)S(1)}, /*index=5*/f...) all-reduce(f32[1024]{0:T(1024)S(1)} %dynamic-update-slice.6, ...), channel_id=1, replica_groups=mesh['dp'=16,'tensor'=2] {'dp','tensor'}, use_global_device_ids=true, to_apply=%add.6 | all-reduce | flops 8192 | bytes 65536
  808.5 25.0 %reduce-scatter.53.cloned.1.call-done = f32[64,512]{1,0:T(8,128)} async-done(((f32[1024,512]{1,0:T(8,128)}), f32[64,512]{1,0:T(8,128)}) %reduce-scatter.53.cloned.1.call-update) | async-done | bytes 131088 | tf_op jit(solution)/shard_map/reduce_scatter | solution.py:149
  833.5 64.8 %reduce-scatter.55.cloned.1.call-done = f32[512,64]{0,1:T(8,128)} async-done(((f32[512,1024]{0,1:T(8,128)}), f32[512,64]{0,1:T(8,128)}) %reduce-scatter.55.cloned.1.call-update) | async-done | bytes 131088 | tf_op jit(solution)/shard_map/reduce_scatter | solution.py:151
  898.3 65.4 %reduce-scatter.51.cloned.1.call-done = f32[512,64]{0,1:T(8,128)} async-done(((f32[512,1024]{0,1:T(8,128)}), f32[512,64]{0,1:T(8,128)}) %reduce-scatter.51.cloned.1.call-update) | async-done | bytes 131088 | tf_op jit(solution)/shard_map/reduce_scatter | solution.py:148
  963.8 88.6 %reduce-scatter.49.cloned.1.call-done = f32[64,3,512]{2,0,1:T(8,128)} async-done(((f32[1024,3,512]{2,0,1:T(8,128)}), f32[64,3,512]{2,0,1:T(8,128)}) %reduce-scatter.49.cloned.1.call-update) | async-done | bytes 393232 | tf_op jit(solution)/shard_map/reduce_scatter | solution.py:147
  1052.4 183.0 %reduce-scatter.59.cloned.1.call-done = f32[256,1024]{1,0:T(8,128)} async-done(((f32[4096,1024]{1,0:T(8,128)}), f32[256,1024]{1,0:T(8,128)}) %reduce-scatter.59.cloned.1.call-update) | async-done | bytes 1048592 | tf_op jit(solution)/shard_map/reduce_scatter | solution.py:154
  1235.5 182.8 %reduce-scatter.57.cloned.1.call-done = f32[1024,256]{1,0:T(8,128)} async-done(((f32[1024,4096]{1,0:T(8,128)}), f32[1024,256]{1,0:T(8,128)}) %reduce-scatter.57.cloned.1.call-update) | async-done | bytes 1048592 | tf_op jit(solution)/shard_map/reduce_scatter | solution.py:152
  (474 shorter events, 159.0 us)
Async XLA Ops:
  7.2 62.2 %all-gather.13.cloned.1.call-start = ((), (), s32[]{:S(2)}) async-start(), calls=%async_computation.20 | async-start | bytes 3342336 | tf_op jit(solution)/shard_map/all_gather | solution.py:207
  7.9 89.5 %all-gather.15.cloned.1.call-start = ((), (), s32[]{:S(2)}) async-start(), calls=%async_computation.21 | async-start | bytes 1114112 | tf_op jit(solution)/shard_map/all_gather | solution.py:208
  8.7 105.1 %reduce-scatter.21.cloned.1.call-start = ((), (), s32[]{:S(2)}) async-start(), calls=%async_computation.22 | async-start | bytes 786432 | tf_op jit(solution)/shard_map/reduce_scatter | solution.py:130
  9.9 62.4 %copy-start.97 = (f32[128]{0:T(128)}, f32[128]{0:T(128)S(1)}, u32[]{:S(2)}) copy-start(f32[128]{0:T(128)S(1)} %broadcast_multiply_fusion.17) | copy-start | bytes 1540
  11.1 61.4 %copy-start.107 = (f32[128]{0:T(128)}, f32[128]{0:T(128)S(1)}, u32[]{:S(2)}) copy-start(f32[128]{0:T(128)S(1)} %add_rsqrt_fusion.5) | copy-start | bytes 1540
  59.0 56.4 %copy-start.77 = (f32[1024]{0:T(1024)}, f32[1024]{0:T(1024)S(1)}, u32[]{:S(2)}) copy-start(f32[1024]{0:T(1024)S(1)} %get-tuple-element.317) | copy-start | bytes 12292
  59.0 117.6 %copy-start.80 = (f32[1024]{0:T(1024)}, f32[1024]{0:T(1024)S(1)}, u32[]{:S(2)}) copy-start(f32[1024]{0:T(1024)S(1)} %get-tuple-element.315) | copy-start | bytes 12292
  59.0 246.9 %copy-start.79 = (f32[1024]{0:T(1024)}, f32[1024]{0:T(1024)S(1)}, u32[]{:S(2)}) copy-start(f32[1024]{0:T(1024)S(1)} %get-tuple-element.319) | copy-start | bytes 12292
  73.7 26.3 %copy-start.73 = (bf16[64,2,512]{2,1,0:T(2,128)(2,1)S(1)}, bf16[64,2,512]{2,1,0:T(2,128)(2,1)}, u32[]{:S(2)}) copy-start(bf16[64,2,512]{2,1,0:T(2,128)(2,1)} %param.27) | copy-start | bytes 393220
  73.7 40.0 %copy-start = (bf16[2,128,1024]{2,1,0:T(8,128)(2,1)S(1)}, bf16[2,128,1024]{2,1,0:T(8,128)(2,1)}, u32[]{:S(2)}) copy-start(bf16[2,128,1024]{2,1,0:T(8,128)(2,1)} %param.20) | copy-start | bytes 1572868
  74.3 53.2 %copy-start.70 = (bf16[8,64,256]{2,1,0:T(8,128)(2,1)}, bf16[8,64,256]{2,1,0:T(8,128)(2,1)S(1)}, u32[]{:S(2)}) copy-start(bf16[8,64,256]{2,1,0:T(8,128)(2,1)S(1)} %convolution_convert_fusion.25) | copy-start | bytes 786436
  99.9 58.1 %all-gather.17.cloned.1.call-start = ((), (), s32[]{:S(2)}) async-start(), calls=%async_computation.23 | async-start | bytes 2228224 | tf_op jit(solution)/shard_map/all_gather | solution.py:210
  100.7 73.4 %reduce-scatter.27.cloned.1.call-start = ((), (), s32[]{:S(2)}) async-start(), calls=%async_computation.30 | async-start | bytes 786432 | tf_op jit(solution)/shard_map/reduce_scatter | solution.py:130
  100.8 27.5 %copy-start.101 = (f32[128]{0:T(128)}, f32[128]{0:T(128)S(1)}, u32[]{:S(2)}) copy-start(f32[128]{0:T(128)S(1)} %broadcast_multiply_fusion.14) | copy-start | bytes 1540
  115.4 13.0 copy-start.109
  133.7 80.4 %all-gather.19.cloned.1.call-start = ((), (), s32[]{:S(2)}) async-start(), calls=%async_computation.24 | async-start | bytes 1114112 | tf_op jit(solution)/shard_map/all_gather | solution.py:209
  134.3 118.9 %all-gather.21.cloned.1.call-start = ((), (), s32[]{:S(2)}) async-start(), calls=%async_computation.25 | async-start | bytes 1114112 | tf_op jit(solution)/shard_map/all_gather | solution.py:211
  135.0 168.9 %reduce-scatter.29.cloned.1.call-start = ((), (), s32[]{:S(2)}) async-start(), calls=%async_computation.31 | async-start | bytes 786432 | tf_op jit(solution)/shard_map/reduce_scatter | solution.py:130
  136.1 38.0 %copy-start.15 = (bf16[128,1024]{1,0:T(8,128)(2,1)S(1)}, bf16[128,1024]{1,0:T(8,128)(2,1)}, u32[]{:S(2)}) copy-start(bf16[128,1024]{1,0:T(8,128)(2,1)} %reduce-scatter.21.cloned.1.call-done) | copy-start | bytes 786436
  141.9 33.5 %copy-start.38 = (bf16[1,128,1024]{2,1,0:T(8,128)(2,1)}, bf16[1,128,1024]{2,1,0:T(8,128)(2,1)S(1)}, u32[]{:S(2)}) copy-start(bf16[1,128,1024]{2,1,0:T(8,128)(2,1)S(1)} %all-gather) | copy-start | bytes 786436
  147.5 27.8 %copy-start.36 = (bf16[1,128,1024]{2,1,0:T(8,128)(2,1)}, bf16[1,128,1024]{2,1,0:T(8,128)(2,1)S(1)}, u32[]{:S(2)}) copy-start(bf16[1,128,1024]{2,1,0:T(8,128)(2,1)S(1)} %all-gather.1) | copy-start | bytes 786436
  187.2 46.3 %copy-start.17 = (bf16[256,1024]{1,0:T(8,128)(2,1)}, bf16[256,1024]{1,0:T(8,128)(2,1)S(1)}, u32[]{:S(2)}) copy-start(bf16[256,1024]{1,0:T(8,128)(2,1)S(1)} %all_gather.130) | copy-start | bytes 1572868
  255.8 48.1 %reduce-scatter.23.cloned.1.call-start = ((), (), s32[]{:S(2)}) async-start(), calls=%async_computation.26 | async-start | bytes 786432 | tf_op jit(solution)/shard_map/reduce_scatter | solution.py:130
  260.2 25.9 %copy-start.25 = (bf16[2,128,1024]{2,1,0:T(8,128)(2,1)S(1)}, bf16[2,128,1024]{2,1,0:T(8,128)(2,1)}, u32[]{:S(2)}) copy-start(bf16[2,128,1024]{2,1,0:T(8,128)(2,1)} %param.39) | copy-start | bytes 1572868
  264.1 42.0 %copy-start.111 = (f32[1024]{0:T(1024)S(1)}, f32[1024]{0:T(1024)}, u32[]{:S(2)}) copy-start(f32[1024]{0:T(1024)} %get-tuple-element.318) | copy-start | bytes 12292
  264.1 104.6 %all-gather.23.cloned.1.call-start = ((), (), s32[]{:S(2)}) async-start(), calls=%async_computation.27 | async-start | bytes 8912896 | tf_op jit(solution)/shard_map/all_gather | solution.py:212
  264.7 179.3 %all-gather.25.cloned.1.call-start = ((), (), s32[]{:S(2)}) async-start(), calls=%async_computation.28 | async-start | bytes 8912896 | tf_op jit(solution)/shard_map/all_gather | solution.py:214
  265.5 212.6 %reduce-scatter.39.cloned.1.call-start = ((), (), s32[]{:S(2)}) async-start(), calls=%async_computation.36 | async-start | bytes 786432 | tf_op jit(solution)/shard_map/reduce_scatter | solution.py:140
  444.0 9.8 copy-start.114
  457.0 30.5 %reduce-scatter.33.cloned.1.call-start = ((), (), s32[]{:S(2)}) async-start(), calls=%async_computation.33 | async-start | bytes 786432 | tf_op jit(solution)/shard_map/reduce_scatter | solution.py:140
  457.5 13.3 slice-start
  473.9 90.5 %reduce-scatter.35.cloned.1.call-start = ((), (), s32[]{:S(2)}) async-start(), calls=%async_computation.34 | async-start | bytes 786432 | tf_op jit(solution)/shard_map/reduce_scatter | solution.py:339
  487.5 14.8 %copy-start.12 = (bf16[512,1024]{0,1:T(8,128)(2,1)S(1)}, bf16[512,1024]{0,1:T(8,128)(2,1)}, u32[]{:S(2)}) copy-start(bf16[512,1024]{0,1:T(8,128)(2,1)} %all-gather.21.cloned.1.call-done) | copy-start | bytes 3145732
  524.6 39.9 %reduce-scatter.41.cloned.1.call-start = ((), (), s32[]{:S(2)}) async-start(), calls=%async_computation.37 | async-start | bytes 786432 | tf_op jit(solution)/shard_map/reduce_scatter | solution.py:339
  531.0 225.7 %reduce-scatter.45.cloned.1.call-start = ((), (), s32[]{:S(2)}) async-start(), calls=%async_computation.39 | async-start | bytes 393216 | tf_op jit(solution)/shard_map/reduce_scatter | solution.py:347
  545.4 211.4 %reduce-scatter.47.cloned.1.call-start = ((), (), s32[]{:S(2)}) async-start(), calls=%async_computation.40 | async-start | bytes 393216 | tf_op jit(solution)/shard_map/reduce_scatter | solution.py:347
  552.4 206.2 %all-reduce.20.cloned.1.call-start = ((), (), s32[]{:S(2)}) async-start(), calls=%async_computation.47 | async-start | bytes 8388608
  564.4 195.9 %reduce-scatter.37.cloned.1.call-start = ((), (), s32[]{:S(2)}) async-start(), calls=%async_computation.35 | async-start | bytes 786432 | tf_op jit(solution)/shard_map/reduce_scatter | solution.py:140
  565.1 12.7 copy-start.8
  610.1 150.2 %reduce-scatter.43.cloned.1.call-start = ((), (), s32[]{:S(2)}) async-start(), calls=%async_computation.38 | async-start | bytes 786432 | tf_op jit(solution)/shard_map/reduce_scatter | solution.py:140
  619.1 12.4 copy-start.62
  623.0 183.2 %reduce-scatter.31.cloned.1.call-start = ((), (), s32[]{:S(2)}) async-start(), calls=%async_computation.32 | async-start | bytes 786432 | tf_op jit(solution)/shard_map/reduce_scatter | solution.py:130
  631.6 9.0 copy-start.18
  631.6 9.0 copy-start.35
  631.6 174.6 %reduce-scatter.25.cloned.1.call-start = ((), (), s32[]{:S(2)}) async-start(), calls=%async_computation.29 | async-start | bytes 786432 | tf_op jit(solution)/shard_map/reduce_scatter | solution.py:130
  640.0 193.6 %reduce-scatter.53.cloned.1.call-start = ((), (), s32[]{:S(2)}) async-start(), calls=%async_computation.43 | async-start | bytes 2228224 | tf_op jit(solution)/shard_map/reduce_scatter | solution.py:149
  642.4 255.9 %reduce-scatter.55.cloned.1.call-start = ((), (), s32[]{:S(2)}) async-start(), calls=%async_computation.44 | async-start | bytes 2228224 | tf_op jit(solution)/shard_map/reduce_scatter | solution.py:151
  645.8 318.0 %reduce-scatter.51.cloned.1.call-start = ((), (), s32[]{:S(2)}) async-start(), calls=%async_computation.42 | async-start | bytes 2228224 | tf_op jit(solution)/shard_map/reduce_scatter | solution.py:148
  649.2 403.2 %reduce-scatter.49.cloned.1.call-start = ((), (), s32[]{:S(2)}) async-start(), calls=%async_computation.41 | async-start | bytes 6684672 | tf_op jit(solution)/shard_map/reduce_scatter | solution.py:147
  655.2 11.9 copy-start.47
  655.2 580.3 %reduce-scatter.59.cloned.1.call-start = ((), (), s32[]{:S(2)}) async-start(), calls=%async_computation.46 | async-start | bytes 17825792 | tf_op jit(solution)/shard_map/reduce_scatter | solution.py:154
  656.2 10.9 copy-start.13
  678.7 739.6 %reduce-scatter.57.cloned.1.call-start = ((), (), s32[]{:S(2)}) async-start(), calls=%async_computation.45 | async-start | bytes 17825792 | tf_op jit(solution)/shard_map/reduce_scatter | solution.py:152
  693.6 63.1 %copy-start.88 = (f32[1024]{0:T(1024)S(1)}, f32[1024]{0:T(1024)}, u32[]{:S(2)}) copy-start(f32[1024]{0:T(1024)} %get-tuple-element.252) | copy-start | bytes 12292
  693.6 63.1 %copy-start.89 = (f32[1024]{0:T(1024)S(1)}, f32[1024]{0:T(1024)}, u32[]{:S(2)}) copy-start(f32[1024]{0:T(1024)} %get-tuple-element.363) | copy-start | bytes 12292
  693.6 63.1 %copy-start.86 = (f32[1024]{0:T(1024)S(1)}, f32[1024]{0:T(1024)}, u32[]{:S(2)}) copy-start(f32[1024]{0:T(1024)} %get-tuple-element.302) | copy-start | bytes 12292
  693.6 63.1 %copy-start.87 = (f32[1024]{0:T(1024)S(1)}, f32[1024]{0:T(1024)}, u32[]{:S(2)}) copy-start(f32[1024]{0:T(1024)} %get-tuple-element.360) | copy-start | bytes 12292
  693.6 66.7 %copy-start.78 = (f32[1024]{0:T(1024)S(1)}, f32[1024]{0:T(1024)}, u32[]{:S(2)}) copy-start(f32[1024]{0:T(1024)} %copy-done.77) | copy-start | bytes 12292
  693.6 66.7 %copy-start.98 = (f32[128]{0:T(128)S(1)}, f32[128]{0:T(128)}, u32[]{:S(2)}) copy-start(f32[128]{0:T(128)} %copy-done.97) | copy-start | bytes 1540
  693.6 66.7 %copy-start.102 = (f32[128]{0:T(128)S(1)}, f32[128]{0:T(128)}, u32[]{:S(2)}) copy-start(f32[128]{0:T(128)} %copy-done.101) | copy-start | bytes 1540
  693.7 66.7 %copy-start.108 = (f32[128]{0:T(128)S(1)}, f32[128]{0:T(128)}, u32[]{:S(2)}) copy-start(f32[128]{0:T(128)} %copy-done.107) | copy-start | bytes 1540
  693.7 66.7 %copy-start.110 = (f32[128]{0:T(128)S(1)}, f32[128]{0:T(128)}, u32[]{:S(2)}) copy-start(f32[128]{0:T(128)} %copy-done.109) | copy-start | bytes 1540
  693.7 109.9 %copy-start.55 = (f32[128,1024]{1,0:T(8,128)S(1)}, f32[128,1024]{1,0:T(8,128)}, u32[]{:S(2)}) copy-start(f32[128,1024]{1,0:T(8,128)} %get-tuple-element.321) | copy-start | bytes 1572868
  696.4 109.9 %copy-start.6 = (f32[128,1024]{1,0:T(8,128)S(1)}, f32[128,1024]{1,0:T(8,128)}, u32[]{:S(2)}) copy-start(f32[128,1024]{1,0:T(8,128)} %copy-done.5) | copy-start | bytes 1572868
  (83 other events, 234.1 us)
Sparse Core Ops, SparseCore 0:
  10.2 48.2 all-gather.12
  60.6 36.7 all-gather.14
  100.2 13.4 reduce-scatter.20
  116.6 41.3 all-gather.16
  160.7 13.3 reduce-scatter.26
  176.1 37.9 all-gather.18
  216.3 36.8 all-gather.20
  256.0 13.4 reduce-scatter.28
  272.4 14.5 reduce-scatter.22
  289.0 79.6 all-gather.22
  370.9 73.0 all-gather.24
  457.1 12.8 reduce-scatter.38
  474.1 13.3 reduce-scatter.32
  524.7 14.5 reduce-scatter.34
  541.5 14.5 reduce-scatter.40
  558.2 11.6 reduce-scatter.44
  572.1 13.0 reduce-scatter.46
  588.7 111.4 all-reduce.19
  702.6 13.4 reduce-scatter.36
  718.2 14.5 reduce-scatter.42
  735.1 14.5 reduce-scatter.30
  751.9 14.5 reduce-scatter.24
  771.3 62.1 reduce-scatter.52
  837.7 60.6 reduce-scatter.54
  903.1 60.6 reduce-scatter.50
  968.1 84.2 reduce-scatter.48
  1057.5 177.9 reduce-scatter.58
  1240.7 177.5 reduce-scatter.56
where the time goes:
time: 1440 us; the launch traced here: 1430 us
  waiting for transfers between devices  834 us (58%)
  blocking collectives  272 us (19%)
  matrix products  185 us (13%)
  local copies, waits for them, and re-layouts  71 us (5%)
  other arithmetic  42.9 us (3%)
  between operations  17.9 us (1%)
    reduce_scatter x1, waiting for transfers between devices, reduce_weights(): lax.psum_scatter(weight_terms[7], 'dp', scatter_dimension=0, tiled=True)  183 us
    reduce_scatter x1, waiting for transfers between devices, reduce_weights(): lax.psum_scatter(weight_terms[5], 'dp', scatter_dimension=1, tiled=True)  183 us
    unnamed x3, blocking collectives  140 us
    reduce_scatter x1, waiting for transfers between devices, reduce_weights(): lax.psum_scatter(weight_terms[0], 'dp', scatter_dimension=0, tiled=True)  88.6 us
    all_gather x1, waiting for transfers between devices, local(): lax.all_gather(hidden_out, 'dp', axis=0, tiled=True)  67.5 us
    reduce_scatter x1, waiting for transfers between devices, reduce_weights(): lax.psum_scatter(weight_terms[1], 'dp', scatter_dimension=1, tiled=True)  65.4 us
    reduce_scatter x1, waiting for transfers between devices, reduce_weights(): lax.psum_scatter(weight_terms[4], 'dp', scatter_dimension=1, tiled=True)  64.8 us
    all_gather x6, blocking collectives, gather_slopes(): return lax.all_gather(local_slopes, 'tensor', axis=0, tiled=True)  50 us
  transfers between devices with their start and end apart: 28, of which 15 were waited for; matrix products, arithmetic and copies ran while one was open for 17% of the time, Pallas kernels for 0%

commit v1 on v0

--- a/solution.py
+++ b/solution.py
@@ -1,13 +1,980 @@
+import functools
+
 import jax
 import jax.numpy as jnp
 from jax import lax
+from jax.experimental import pallas as pl
+from jax.experimental.pallas import tpu as pltpu
 from jax.sharding import PartitionSpec as P
 
 HEAD = 64
-
-
 EPS = 1e-05
 NEGATIVE = -1e30
+MESH = pl.DeviceIdType.MESH
+HBM = pltpu.HBM
+VMEM = pltpu.VMEM
+PIECES = 8
+FF_PIECES = 16
+
+
+class Place:
+    def __init__(self):
+        self.dp = lax.axis_index("dp")
+        self.y = lax.axis_index("tensor")
+        self.c = lax.rem(self.dp, 2)
+        self.x = lax.rem(self.dp // 2, 2)
+        self.z = self.dp // 4
+
+    def at(self, z=None, x=None, c=None, y=None):
+        z = self.z if z is None else z
+        x = self.x if x is None else x
+        c = self.c if c is None else c
+        y = self.y if y is None else y
+        return ((z * 2 + x) * 2 + c, y)
+
+    def core(self):
+        return self.at(c=1 - self.c)
+
+    def xn(self):
+        return self.at(x=1 - self.x)
+
+    def yn(self):
+        return self.at(y=1 - self.y)
+
+    def up(self):
+        return self.at(z=self.z + 1)
+
+    def down(self):
+        return self.at(z=self.z - 1)
+
+
+def remote(src, dst, send, recv, device):
+    return pltpu.make_async_remote_copy(
+        src_ref=src, dst_ref=dst, send_sem=send, recv_sem=recv, device_id=device, device_id_type=MESH
+    )
+
+
+def signal(sem, device):
+    pl.semaphore_signal(sem, inc=1, device_id=device, device_id_type=MESH)
+
+
+class LineGather:
+    def __init__(self, place, depth, slot, send, recv):
+        self.p, self.n, self.slot, self.send, self.recv = place, depth, slot, send, recv
+
+    def _copy_up(self, k):
+        b = self.p.z - k
+        return remote(self.slot(b), self.slot(b), self.send.at[0, k], self.recv.at[0, k], self.p.up())
+
+    def _copy_down(self, k):
+        b = self.p.z + k
+        return remote(self.slot(b), self.slot(b), self.send.at[1, k], self.recv.at[1, k], self.p.down())
+
+    def _from_below(self, k):
+        b = self.p.z - k
+        return remote(self.slot(b), self.slot(b), self.send.at[0, k - 1], self.recv.at[0, k - 1], self.p.up())
+
+    def _from_above(self, k):
+        b = self.p.z + k
+        return remote(self.slot(b), self.slot(b), self.send.at[1, k - 1], self.recv.at[1, k - 1], self.p.down())
+
+    def arrive(self, k):
+        z = self.p.z
+
+        @pl.when(z - k >= 0)
+        def _():
+            self._from_below(k).wait_recv()
+
+        @pl.when(z + k <= self.n - 1)
+        def _():
+            self._from_above(k).wait_recv()
+
+    def step(self, k):
+        z = self.p.z
+        if k > 0:
+            self.arrive(k)
+        if k < self.n - 1:
+
+            @pl.when((z - k >= 0) & (z < self.n - 1))
+            def _():
+                self._copy_up(k).start()
+
+            @pl.when((z + k <= self.n - 1) & (z > 0))
+            def _():
+                self._copy_down(k).start()
+
+    def sent(self):
+        z = self.p.z
+        for k in range(self.n - 1):
+
+            @pl.when((z - k >= 0) & (z < self.n - 1))
+            def _():
+                self._copy_up(k).wait_send()
+
+            @pl.when((z + k <= self.n - 1) & (z > 0))
+            def _():
+                self._copy_down(k).wait_send()
+
+
+class PlaneGather:
+    def __init__(self, place, slot, send, recv):
+        self.p, self.slot, self.send, self.recv = place, slot, send, recv
+        p = place
+        x, y, c = p.x, p.y, p.c
+        ox, oy = 1 - x, 1 - y
+        self.moves = [
+            ((x, c, y, None), p.xn(), 0),
+            ((x, c, y, None), p.yn(), 1),
+            ((ox, c, y, 0), p.yn(), 2),
+            ((x, c, oy, 1), p.xn(), 3),
+            ((x, c, y, None), p.core(), 4),
+            ((ox, c, y, None), p.core(), 5),
+            ((x, c, oy, None), p.core(), 6),
+            ((ox, c, oy, None), p.core(), 7),
+        ]
+        oc = 1 - c
+        self.arrivals = [
+            (ox, c, y, None),
+            (x, c, oy, None),
+            (ox, c, oy, 0),
+            (ox, c, oy, 1),
+            (x, oc, y, None),
+            (ox, oc, y, None),
+            (x, oc, oy, None),
+            (ox, oc, oy, None),
+        ]
+
+    def _move(self, i):
+        where, device, s = self.moves[i]
+        return remote(self.slot(*where), self.slot(*where), self.send.at[s], self.recv.at[s], device)
+
+    def _arrival(self, i):
+        view = self.slot(*self.arrivals[i])
+        return remote(view, view, self.send.at[i], self.recv.at[i], self.moves[i][1])
+
+    def begin(self):
+        self._move(0).start()
+        self._move(1).start()
+        self._move(4).start()
+
+    def forward(self):
+        self._arrival(0).wait_recv()
+        self._move(2).start()
+        self._move(5).start()
+        self._arrival(1).wait_recv()
+        self._move(3).start()
+        self._move(6).start()
+
+    def finish(self):
+        self._arrival(2).wait_recv()
+        self._arrival(3).wait_recv()
+        self._move(7).start()
+
+    def end(self):
+        for i in range(4, 8):
+            self._arrival(i).wait_recv()
+
+    def sent(self):
+        for i in range(8):
+            self._move(i).wait_send()
+
+
+def all_barrier(place, count):
+    sem = pltpu.get_barrier_semaphore()
+    me = place.dp * 2 + place.y
+
+    @pl.loop(1, count)
+    def _(j):
+        other = lax.rem(me + j, count)
+        signal(sem, (other // 2, lax.rem(other, 2)))
+
+    pl.semaphore_wait(sem, count - 1)
+
+
+def gather_kernel(
+    depth,
+    attn_ref, win_ref, wout_ref, vec_ref, tok_ref, enc_ref, cot_ref,
+    G, Win, Wout, vec_all, tok_row, enc_row, g3,
+    lsem, zs, zr, fs, fr, ps, pr, vs, vr, ss, sr,
+):
+    p = Place()
+    count = 8 * depth
+    local = []
+
+    def keep(src, dst):
+        copy = pltpu.make_async_copy(src, dst, lsem.at[len(local)])
+        copy.start()
+        local.append(copy)
+
+    me = p.dp * 2 + p.y
+    keep(attn_ref, G.at[:, p.y, p.z, p.x, p.c])
+    keep(win_ref, Win.at[p.z])
+    keep(wout_ref, Wout.at[p.z])
+    keep(vec_ref, vec_all.at[me])
+    keep(tok_ref.at[p.y], tok_row.at[p.y])
+    keep(enc_ref.at[p.y], enc_row.at[p.y])
+    keep(cot_ref, g3.at[p.x, p.c, :, p.y])
+    all_barrier(p, count)
+    for copy in local:
+        copy.wait()
+
+    lines = []
+    for i in range(PIECES):
+        lines.append(LineGather(p, depth, lambda b, i=i: G.at[i, p.y, b, p.x, p.c], zs.at[i], zr.at[i]))
+    wr = Win.shape[1] // (FF_PIECES // 2)
+    orow = Wout.shape[1] // (FF_PIECES // 2)
+    ff = []
+    for i in range(FF_PIECES):
+        if i < FF_PIECES // 2:
+            slot = lambda b, i=i: Win.at[b, pl.ds(i * wr, wr)]
+        else:
+            slot = lambda b, i=i: Wout.at[b, pl.ds((i - FF_PIECES // 2) * orow, orow)]
+        ff.append(LineGather(p, depth, slot, fs.at[i], fr.at[i]))
+
+    def plane_slot(i):
+        half = G.shape[5] // 2
+
+        def slot(x, c, y, h):
+            if h is None:
+                return G.at[i, y, :, x, c]
+            return G.at[i, y, :, x, c, pl.ds(h * half, half)]
+
+        return slot
+
+    def g3_slot(x, c, y, h):
+        if h is None:
+            return g3.at[x, c, :, y]
+        return g3.at[x, c, h, y]
+
+    planes = [PlaneGather(p, plane_slot(i), ps.at[i], pr.at[i]) for i in range(PIECES)]
+    planes.append(PlaneGather(p, g3_slot, ps.at[PIECES], pr.at[PIECES]))
+    swaps = [
+        remote(tok_ref.at[1 - p.y], tok_row.at[p.y], ss.at[0], sr.at[0], p.yn()),
+        remote(enc_ref.at[1 - p.y], enc_row.at[p.y], ss.at[1], sr.at[1], p.yn()),
+    ]
+    swaps[0].start()
+
+    @pl.loop(1, count)
+    def _(j):
+        other = lax.rem(me + j, count)
+        remote(vec_ref, vec_all.at[me], vs.at[j], vr.at[j], (other // 2, lax.rem(other, 2))).start()
+
+    swaps[1].start()
+    total = max(PIECES + 1 + depth + 3, FF_PIECES + depth)
+    for it in range(total):
+        for k in range(depth):
+            if 0 <= it - k < PIECES:
+                lines[it - k].step(k)
+        for k in range(depth):
+            if 0 <= it - k < FF_PIECES:
+                ff[it - k].step(k)
+        j = it - (depth - 1)
+        if 0 <= j < PIECES + 1:
+            planes[j].begin()
+        if 0 <= j - 1 < PIECES + 1:
+            planes[j - 1].forward()
+        if 0 <= j - 2 < PIECES + 1:
+            planes[j - 2].finish()
+        if 0 <= j - 3 < PIECES + 1:
+            planes[j - 3].end()
+    for line in lines + ff:
+        line.sent()
+    for plane in planes:
+        plane.sent()
+    for copy in swaps:
+        copy.wait()
+
+    @pl.loop(1, count)
+    def _(j):
+        other = lax.rem(me + j, count)
+        source = lax.rem(me + count - j, count)
+        copy = remote(vec_ref, vec_all.at[source], vs.at[j], vr.at[j], (other // 2, lax.rem(other, 2)))
+        copy.wait()
+
+
+def gather_all(attn, win, wout, vec, tok, enc, cot):
+    depth = lax.axis_size("dp") // 4
+    rows, cols = attn.shape[1:]
+    bf = jnp.bfloat16
+    count = 8 * depth
+    d = tok.shape[2]
+    out_shape = [
+        jax.ShapeDtypeStruct((PIECES, 2, depth, 2, 2, rows, cols), bf),
+        jax.ShapeDtypeStruct((depth,) + win.shape, bf),
+        jax.ShapeDtypeStruct((depth,) + wout.shape, bf),
+        jax.ShapeDtypeStruct((count,) + vec.shape, jnp.float32),
+        jax.ShapeDtypeStruct(tok.shape, bf),
+        jax.ShapeDtypeStruct(enc.shape, bf),
+        jax.ShapeDtypeStruct((2, 2, 2, 2) + cot.shape[1:], bf),
+    ]
+    dma = pltpu.SemaphoreType.DMA
+    return pl.pallas_call(
+        functools.partial(gather_kernel, depth),
+        out_shape=out_shape,
+        in_specs=[pl.BlockSpec(memory_space=VMEM)] * 7,
+        out_specs=[pl.BlockSpec(memory_space=HBM)] * 7,
+        scratch_shapes=[
+            dma((7,)),
+            dma((PIECES, 2, depth - 1)), dma((PIECES, 2, depth - 1)),
+            dma((FF_PIECES, 2, depth - 1)), dma((FF_PIECES, 2, depth - 1)),
+            dma((PIECES + 1, 8)), dma((PIECES + 1, 8)),
+            dma((count,)), dma((count,)),
+            dma((2,)), dma((2,)),
+        ],
+        compiler_params=pltpu.CompilerParams(
+            collective_id=1, has_side_effects=True, vmem_limit_bytes=24 << 20
+        ),
+        name="gather_all",
+    )(attn, win, wout, vec, tok, enc, cot)
+
+
+def far_first(z, s, depth):
+    b = 0
+    for place in range(depth):
+        order = sorted(range(depth), key=lambda k: (-abs(k - place), k))
+        b = jnp.where(z == place, order[s], b)
+    return b
+
+
+class LineReduce:
+    def __init__(self, place, depth, part, slots, send, recv):
+        self.p, self.n, self.part, self.slots, self.send, self.recv = place, depth, part, slots, send, recv
+
+    def _up(self, b):
+        slot = b - (self.p.z + 1)
+        return remote(self.part(b), self.slots(slot), self.send.at[b], self.recv.at[slot], self.p.up())
+
+    def _down(self, b):
+        slot = self.n - b
+        return remote(self.part(b), self.slots(slot), self.send.at[b], self.recv.at[slot], self.p.down())
+
+    def below(self, b):
+        slot = b - self.p.z
+        return remote(self.slots(slot), self.slots(slot), self.send.at[b], self.recv.at[slot], self.p.up())
+
+    def above(self, b):
+        slot = self.n - b
+        return remote(self.slots(slot), self.slots(slot), self.send.at[b], self.recv.at[slot], self.p.down())
+
+    def first(self, b):
+        z = self.p.z
+
+        @pl.when((z == 0) & (b > z))
+        def _():
+            self._up(b).start()
+
+        @pl.when((z == self.n - 1) & (b < z))
+        def _():
+            self._down(b).start()
+
+    def middle(self, b, add):
+        z = self.p.z
+
+        @pl.when((z > 0) & (b > z))
+        def _():
+            self.below(b).wait_recv()
+            add(self.part(b), self.slots(b - z))
+            self._up(b).start()
+
+        @pl.when((z < self.n - 1) & (b < z))
+        def _():
+            self.above(b).wait_recv()
+            add(self.part(b), self.slots(self.n - b))
+            self._down(b).start()
+
+    def last(self, take):
+        z = self.p.z
+
+        @pl.when(z > 0)
+        def _():
+            self.below(z).wait_recv()
+            take(self.slots(0))
+
+        @pl.when(z < self.n - 1)
+        def _():
+            self.above(z).wait_recv()
+            take(self.slots(self.n - z))
+
+    def sent(self):
+        z = self.p.z
+
+        @pl.loop(0, self.n)
+        def _(b):
+            @pl.when(b > z)
+            def _():
+                self._up(b).wait_send()
+
+            @pl.when(b < z)
+            def _():
+                self._down(b).wait_send()
+
+
+def add_low(part, other):
+    part[...] = (part[...].astype(jnp.float32) + other[...].astype(jnp.float32)).astype(part.dtype)
+
+
+def gelu_pair(x):
+    a, b = 0.7978845608028654, 0.044715
+    square = x * x
+    t = jnp.tanh(a * x * (1.0 + b * square))
+    half = 0.5 * (1.0 + t)
+    return x * half, half + 0.5 * x * (1.0 - t * t) * (a * (1.0 + 3.0 * b * square))
+
+
+NN = (((1,), (0,)), ((), ()))
+NT = (((1,), (1,)), ((), ()))
+TN = (((0,), (0,)), ((), ()))
+
+
+def mm(left, right, form=NN):
+    return lax.dot_general(left, right, form, preferred_element_type=jnp.float32)
+
+
+def neighbour_barrier(p, depth):
+    sem = pltpu.get_barrier_semaphore()
+    for dx in range(2):
+        for dc in range(2):
+            for dy in range(2):
+                if dx + dc + dy:
+                    signal(sem, p.at(x=lax.rem(p.x + dx, 2), c=lax.rem(p.c + dc, 2), y=lax.rem(p.y + dy, 2)))
+
+    @pl.loop(1, depth)
+    def _(k):
+        signal(sem, p.at(z=lax.rem(p.z + k, depth)))
+
+    pl.semaphore_wait(sem, 7 + depth - 1)
+
+
+def hidden_kernel(
+    depth,
+    hn_ref, bias_ref, Win, Wout, g3,
+    y_out, d_out, gin_out, gout_out, gbias_out,
+    HN, G3, WI, WO, Y, D, S, R, acc_in, acc_out, BS, BR, CS, CR, PS, PR,
+    lsem, ps, pr, zs, zr, bs, br, cs, cr, xs, xr,
+):
+    p = Place()
+    rows = HN.shape[3]
+    width = HN.shape[4]
+    loads = [
+        pltpu.make_async_copy(Win, WI, lsem.at[0]),
+        pltpu.make_async_copy(Wout, WO, lsem.at[1]),
+        pltpu.make_async_copy(g3, G3, lsem.at[2]),
+    ]
+    for load in loads:
+        load.start()
+    neighbour_barrier(p, depth)
+    HN[p.x, p.c, p.y] = hn_ref[...]
+    half = rows // 2
+
+    def hn_slot(x, c, y, h):
+        if h is None:
+            return HN.at[x, c, y]
+        return HN.at[x, c, y, pl.ds(h * half, half)]
+
+    gather = PlaneGather(p, hn_slot, ps, pr)
+    gather.begin()
+    Y[...] = jnp.zeros_like(Y)
+    D[...] = jnp.zeros_like(D)
+    BS[...] = jnp.zeros_like(BS)
+    for load in loads:
+        load.wait()
+    gather.forward()
+    gather.finish()
+    gather.end()
+
+    def where(i):
+        dc = 1 - i // 4
+        dx = 1 - lax.rem(i, 4) // 2
+        dy = 1 - lax.rem(i, 2)
+        return lax.rem(p.x + dx, 2), lax.rem(p.c + dc, 2), lax.rem(p.y + dy, 2)
+
+    def one_row(b, i, first):
+        at = where(i)
+        h = HN[at]
+        g = G3[at].reshape(rows, width)
+        win, wout = WI[b], WO[b]
+        before = mm(h, win) + bias_ref[b]
+        active, slope = gelu_pair(before)
+        active = active.astype(jnp.bfloat16)
+        slope = (mm(g, wout, NT) * slope).astype(jnp.bfloat16)
+        Y[at] += mm(active, wout)
+        D[at] += mm(slope, win, NT)
+        acc_out[...] += mm(active, g, TN)
+        acc_in[...] += mm(slope, h, TN)
+        BS[b, 0:1] += jnp.sum(slope.astype(jnp.float32), axis=0, keepdims=True)
+
+    reduce = LineReduce(p, depth, lambda b: S.at[b], lambda i: R.at[i], zs, zr)
+
+    def open_block():
+        acc_in[...] = jnp.zeros_like(acc_in)
+        acc_out[...] = jnp.zeros_like(acc_out)
+
+    def close_block(b):
+        S[b, 0] = acc_in[...].astype(jnp.bfloat16)
+        S[b, 1] = acc_out[...].astype(jnp.bfloat16)
+
+    for s in range(depth - 1):
+        b = far_first(p.z, s, depth)
+        open_block()
+
+        @pl.loop(0, 8)
+        def _(i):
+            one_row(b, i, False)
+
+        close_block(b)
+        reduce.first(b)
+        remote(BS.at[b], BR.at[p.z], bs.at[b], br.at[p.z], p.at(z=b)).start()
+
+    b = p.z
+    open_block()
+
+    def to_core(j):
+        return remote(CS.at[j], CR.at[j], cs.at[j], cr.at[j], p.core())
+
+    def to_chip(j):
+        dx, dy = 1 - j // 2, 1 - lax.rem(j, 2)
+        return remote(
+            PS.at[j], PR.at[j], xs.at[j], xr.at[j], p.at(x=lax.rem(p.x + dx, 2), y=lax.rem(p.y + dy, 2))
+        )
+
+    @pl.loop(0, 4)
+    def _(i):
+        one_row(b, i, False)
+        at = where(i)
+        CS[i, 0] = D[at].astype(jnp.bfloat16)
+        CS[i, 1] = Y[at].astype(jnp.bfloat16)
+        to_core(i).start()
+
+    @pl.loop(4, 8)
+    def _(i):
+        one_row(b, i, False)
+        at = where(i)
+        j = i - 4
+        to_core(j).wait_recv()
+        dsum = D[at] + CR[j, 0].astype(jnp.float32)
+        ysum = Y[at] + CR[j, 1].astype(jnp.float32)
+
+        @pl.when(i < 7)
+        def _():
+            PS[j, 0] = dsum.astype(jnp.bfloat16)
+            PS[j, 1] = ysum.astype(jnp.bfloat16)
+            to_chip(j).start()
+
+        @pl.when(i == 7)
+        def _():
+            d_out[...] = dsum
+            y_out[...] = ysum
+
+    gin_out[...] = acc_in[...]
+    gout_out[...] = acc_out[...]
+
+    @pl.loop(0, 3)
+    def _(j):
+        to_chip(j).wait_recv()
+        d_out[...] += PR[j, 0].astype(jnp.float32)
+        y_out[...] += PR[j, 1].astype(jnp.float32)
+
+    for s in range(depth - 1):
+        reduce.middle(far_first(p.z, s, depth), add_low)
+
+    def take(slot):
+        gin_out[...] += slot[0].astype(jnp.float32)
+        gout_out[...] += slot[1].astype(jnp.float32)
+
+    reduce.last(take)
+    gbias_out[...] = BS[p.z]
+
+    @pl.loop(1, depth)
+    def _(k):
+        source = lax.rem(p.z + k, depth)
+        remote(BS.at[source], BR.at[source], bs.at[source], br.at[source], p.at(z=source)).wait()
+        gbias_out[...] += BR[source]
+
+    reduce.sent()
+    gather.sent()
+
+    @pl.loop(0, 4)
+    def _(j):
+        to_core(j).wait_send()
+
+    @pl.loop(0, 3)
+    def _(j):
+        to_chip(j).wait_send()
+
+
+def hidden_block(hn, bias, win, wout, g3):
+    depth, width, units = win.shape
+    rows = hn.shape[0]
+    bf, f32 = jnp.bfloat16, jnp.float32
+    dma = pltpu.SemaphoreType.DMA
+    vm = pl.BlockSpec(memory_space=VMEM)
+    hb = pl.BlockSpec(memory_space=HBM)
+    return pl.pallas_call(
+        functools.partial(hidden_kernel, depth),
+        out_shape=[
+            jax.ShapeDtypeStruct((rows, width), f32),
+            jax.ShapeDtypeStruct((rows, width), f32),
+            jax.ShapeDtypeStruct((units, width), f32),
+            jax.ShapeDtypeStruct((units, width), f32),
+            jax.ShapeDtypeStruct((8, units), f32),
+        ],
+        in_specs=[vm, vm, hb, hb, hb],
+        out_specs=[vm] * 5,
+        scratch_shapes=[
+            pltpu.VMEM((2, 2, 2, rows, width), bf),
+            pltpu.VMEM(g3.shape, bf),
+            pltpu.VMEM(win.shape, bf),
+            pltpu.VMEM(wout.shape, bf),
+            pltpu.VMEM((2, 2, 2, rows, width), f32),
+            pltpu.VMEM((2, 2, 2, rows, width), f32),
+            pltpu.VMEM((depth, 2, units, width), bf),
+            pltpu.VMEM((depth + 1, 2, units, width), bf),
+            pltpu.VMEM((units, width), f32),
+            pltpu.VMEM((units, width), f32),
+            pltpu.VMEM((depth, 8, units), f32),
+            pltpu.VMEM((depth, 8, units), f32),
+            pltpu.VMEM((4, 2, rows, width), bf),
+            pltpu.VMEM((4, 2, rows, width), bf),
+            pltpu.VMEM((3, 2, rows, width), bf),
+            pltpu.VMEM((3, 2, rows, width), bf),
+            dma((3,)),
+            dma((8,)), dma((8,)),
+            dma((depth,)), dma((depth + 1,)),
+            dma((depth,)), dma((depth,)),
+            dma((4,)), dma((4,)),
+            dma((3,)), dma((3,)),
+        ],
+        compiler_params=pltpu.CompilerParams(
+            collective_id=2, has_side_effects=True, vmem_limit_bytes=62 << 20
+        ),
+        name="hidden_block",
+    )(hn, bias, win, wout, g3)
+
+
+def reduce_kernel(
+    depth,
+    part, vec_ref, res_ref, tg_ref, eg_ref,
+    gw_out, vec_out, res_out, tg_out, eg_out,
+    MY, CR, PD, PR, R, VR, XS, XR, ES, ER,
+    lsem, cs, cr, ds, dr, ps, pr, zs, zr, vs, vr, ss, sr,
+):
+    p = Place()
+    count = 8 * depth
+    me = p.dp * 2 + p.y
+    ox, oy, oc = 1 - p.x, 1 - p.y, 1 - p.c
+    half = MY.shape[4] // 2
+    all_barrier(p, count)
+
+    @pl.loop(1, count)
+    def _(j):
+        other = lax.rem(me + j, count)
+        remote(vec_ref.at[other], VR.at[j], vs.at[j], vr.at[j], (other // 2, lax.rem(other, 2))).start()
+
+    rows = res_out.shape[1]
+    short = eg_out.shape[1]
+    XS[0] = res_ref[pl.ds(oy * rows, rows)].astype(jnp.bfloat16)
+    XS[1] = tg_ref[pl.ds(oy * rows, rows)].astype(jnp.bfloat16)
+    ES[...] = eg_ref[pl.ds(oy * short, short)].astype(jnp.bfloat16)
+    swaps = [
+        remote(XS, XR, ss.at[0], sr.at[0], p.yn()),
+        remote(ES, ER, ss.at[1], sr.at[1], p.yn()),
+    ]
+
+    def load(i):
+        return pltpu.make_async_copy(part.at[i, :, :, :, p.c], MY.at[i], lsem.at[i])
+
+    def core(i):
+        return remote(part.at[i, :, :, :, oc], CR.at[i], cs.at[i], cr.at[i], p.core())
+
+    def diagonal(i, h):
+        return remote(
+            MY.at[i, oy, :, ox, pl.ds(h * half, half)], PD.at[i, h], ds.at[i, h], dr.at[i, h],
+            p.yn() if h else p.xn(),
+        )
+
+    def column(i, h):
+        view = MY.at[i, oy, :, p.x] if h else MY.at[i, p.y, :, ox]
+        return remote(view, PR.at[i, h], ps.at[i, h], pr.at[i, h], p.yn() if h else p.xn())
+
+    lines = [
+        LineReduce(
+            p, depth, lambda b, i=i: MY.at[i, p.y, b, p.x], lambda k, i=i: R.at[i, k], zs.at[i], zr.at[i]
+        )
+        for i in range(PIECES)
+    ]
+
+    def stage(i, s):
+        if s == 0:
+            load(i).start()
+            core(i).start()
+        elif s == 1:
+            load(i).wait()
+            core(i).wait_recv()
+            add_low(MY.at[i], CR.at[i])
+            diagonal(i, 0).start()
+            diagonal(i, 1).start()
+        elif s == 2:
+            diagonal(i, 0).wait_recv()
+            add_low(MY.at[i, oy, :, p.x, pl.ds(0, half)], PD.at[i, 0])
+            column(i, 1).start()
+            diagonal(i, 1).wait_recv()
+            add_low(MY.at[i, p.y, :, ox, pl.ds(half, half)], PD.at[i, 1])
+            column(i, 0).start()
+        elif s == 3:
+            column(i, 0).wait_recv()
+            column(i, 1).wait_recv()
+            view = MY.at[i, p.y, :, p.x]
+            view[...] = (
+                view[...].astype(jnp.float32)
+                + PR[i, 0].astype(jnp.float32)
+                + PR[i, 1].astype(jnp.float32)
+            ).astype(jnp.bfloat16)
+            for k in range(depth - 1):
+                lines[i].first(far_first(p.z, k, depth))
+        elif s < 3 + depth:
+            lines[i].middle(far_first(p.z, s - 4, depth), add_low)
+        elif s == 3 + depth:
+            gw_out[i] = MY[i, p.y, p.z, p.x].astype(jnp.float32)
+
+            def take(slot):
+                gw_out[i] += slot[...].astype(jnp.float32)
+
+            lines[i].last(take)
+
+    for it in range(PIECES + 3 + depth):
+        for s in range(4 + depth):
+            if 0 <= it - s < PIECES:
+                stage(it - s, s)
+    swaps[0].start()
+    swaps[1].start()
+    vec_out[...] = vec_ref[me]
+
+    @pl.loop(1, count)
+    def _(j):
+        other = lax.rem(me + j, count)
+        remote(vec_ref.at[other], VR.at[j], vs.at[j], vr.at[j], (other // 2, lax.rem(other, 2))).wait()
+        vec_out[...] += VR[j]
+
+    res_out[p.y] = res_ref[pl.ds(p.y * rows, rows)]
+    tg_out[p.y] = tg_ref[pl.ds(p.y * rows, rows)]
+    eg_out[p.y] = eg_ref[pl.ds(p.y * short, short)]
+    for copy in swaps:
+        copy.wait()
+    res_out[oy] = XR[0].astype(jnp.float32)
+    tg_out[oy] = XR[1].astype(jnp.float32)
+    eg_out[oy] = ER[...].astype(jnp.float32)
+    for i in range(PIECES):
+        core(i).wait_send()
+        for h in range(2):
+            diagonal(i, h).wait_send()
+            column(i, h).wait_send()
+        lines[i].sent()
+
+
+def reduce_all(part, vec, res, tg, eg):
+    depth = part.shape[2]
+    count = 8 * depth
+    rows, cols = part.shape[5:]
+    length, width = res.shape
+    short = eg.shape[0]
+    bf, f32 = jnp.bfloat16, jnp.float32
+    dma = pltpu.SemaphoreType.DMA
+    vm = pl.BlockSpec(memory_space=VMEM)
+    hb = pl.BlockSpec(memory_space=HBM)
+    return pl.pallas_call(
+        functools.partial(reduce_kernel, depth),
+        out_shape=[
+            jax.ShapeDtypeStruct((PIECES, rows, cols), f32),
+            jax.ShapeDtypeStruct(vec.shape[1:], f32),
+            jax.ShapeDtypeStruct((2, length // 2, width), f32),
+            jax.ShapeDtypeStruct((2, length // 2, width), f32),
+            jax.ShapeDtypeStruct((2, short // 2, width), f32),
+        ],
+        in_specs=[hb, vm, vm, vm, vm],
+        out_specs=[vm] * 5,
+        scratch_shapes=[
+            pltpu.VMEM((PIECES, 2, depth, 2, rows, cols), bf),
+            pltpu.VMEM((PIECES, 2, depth, 2, rows, cols), bf),
+            pltpu.VMEM((PIECES, 2, depth, rows // 2, cols), bf),
+            pltpu.VMEM((PIECES, 2, depth, rows, cols), bf),
+            pltpu.VMEM((PIECES, depth + 1, rows, cols), bf),
+            pltpu.VMEM(vec.shape, f32),
+            pltpu.VMEM((2, length // 2, width), bf),
+            pltpu.VMEM((2, length // 2, width), bf),
+            pltpu.VMEM((short // 2, width), bf),
+            pltpu.VMEM((short // 2, width), bf),
+            dma((PIECES,)),
+            dma((PIECES,)), dma((PIECES,)),
+            dma((PIECES, 2)), dma((PIECES, 2)),
+            dma((PIECES, 2)), dma((PIECES, 2)),
+            dma((PIECES, depth)), dma((PIECES, depth + 1)),
+            dma((count,)), dma((count,)),
+            dma((2,)), dma((2,)),
+        ],
+        compiler_params=pltpu.CompilerParams(
+            collective_id=3, has_side_effects=True, vmem_limit_bytes=56 << 20
+        ),
+        name="reduce_all",
+    )(part, vec, res, tg, eg)
+
+
+def norm_forward(hidden, gain, shift):
+    center = hidden - jnp.mean(hidden, axis=-1, keepdims=True)
+    inverse = lax.rsqrt(jnp.mean(center * center, axis=-1, keepdims=True) + EPS)
+    normal = center * inverse
+    return normal * gain + shift, normal, inverse
+
+
+def norm_backward(upward, normal, inverse, gain):
+    scaled = upward * gain
+    centred = (
+        scaled
+        - jnp.mean(scaled, axis=-1, keepdims=True)
+        - normal * jnp.mean(scaled * normal, axis=-1, keepdims=True)
+    )
+    return centred * inverse, jnp.sum(upward * normal, axis=0), jnp.sum(upward, axis=0)
+
+
+def split_heads(a):
+    return a.reshape(a.shape[0], -1, HEAD)
+
+
+def ein(form, *operands):
+    return jnp.einsum(form, *operands, preferred_element_type=jnp.float32)
+
+
+def attend(q, k, v, allowed):
+    scores = ein("qhd,khd->hqk", split_heads(q), split_heads(k)) * HEAD**-0.5
+    scores = jnp.where(allowed[None], scores, NEGATIVE)
+    highest = jnp.max(scores, axis=-1, keepdims=True)
+    exponent = jnp.exp(scores - highest)
+    totals = jnp.sum(exponent, axis=-1, keepdims=True)
+    probs = exponent / totals
+    mixture = ein("hqk,khd->qhd", probs.astype(jnp.bfloat16), split_heads(v))
+    return mixture.reshape(q.shape).astype(jnp.bfloat16), highest + jnp.log(totals)
+
+
+def attend_backward(q, k, v, allowed, lse, slope):
+    scores = ein("qhd,khd->hqk", split_heads(q), split_heads(k)) * HEAD**-0.5
+    scores = jnp.where(allowed[None], scores, NEGATIVE)
+    probs = jnp.exp(scores - lse)
+    up = split_heads(slope)
+    dprobs = ein("qhd,khd->hqk", up, split_heads(v))
+    dscores = (probs * (dprobs - jnp.sum(probs * dprobs, axis=-1, keepdims=True))).astype(jnp.bfloat16)
+    dq = (ein("hqk,khd->qhd", dscores, split_heads(k)) * HEAD**-0.5).astype(jnp.bfloat16)
+    dk = (ein("hqk,qhd->khd", dscores, split_heads(q)) * HEAD**-0.5).astype(jnp.bfloat16)
+    dv = ein("hqk,qhd->khd", probs.astype(jnp.bfloat16), up).astype(jnp.bfloat16)
+    return dq.reshape(q.shape), dk.reshape(k.shape), dv.reshape(v.shape)
+
+
+def fast_local(
+    tokens, encoder, target_doc, source_doc, self_proj, self_out, cross_query, cross_pairs, cross_out,
+    hidden_in, hidden_in_bias, hidden_out, hidden_out_bias, self_gain, self_shift, cross_gain, cross_shift,
+    hidden_gain, hidden_shift, cotangent,
+):
+    depth = lax.axis_size("dp") // 4
+    count = 8 * depth
+    place = Place()
+    me = place.dp * 2 + place.y
+    bf, f32 = jnp.bfloat16, jnp.float32
+    attn = jnp.stack([
+        self_proj[:, 0], self_proj[:, 1], self_proj[:, 2], self_out.T,
+        cross_pairs[:, 0], cross_pairs[:, 1], cross_query, cross_out.T,
+    ])
+    vectors = jnp.stack(
+        [self_gain, self_shift, cross_gain, cross_shift, hidden_gain, hidden_shift, hidden_out_bias]
+    )
+    span = vectors.shape[1]
+    group = 128 // span
+    lane = lax.broadcasted_iota(jnp.int32, (1, 128), 1)
+    mine = lane // span == lax.rem(me, group)
+    vec = jnp.concatenate([
+        jnp.where(mine, jnp.tile(vectors, (1, group)), 0.0),
+        jnp.zeros((1, 128), f32),
+        hidden_in_bias.astype(f32).reshape(-1, 128),
+    ])
+    vec = jnp.pad(vec, ((0, -vec.shape[0] % 8), (0, 0)))
+    G, win, wout, vec_all, tok_row, enc_row, g3 = gather_all(
+        attn, hidden_in, hidden_out, vec, tokens, encoder, cotangent
+    )
+    full = vec_all[:, :7].reshape(count // group, group, 7, 128).sum(1).transpose(1, 0, 2).reshape(7, -1)
+    sg, ss, cg, cs, hg, hs, ob = [full[i] for i in range(7)]
+    units = hidden_in.shape[1]
+    bias = vec_all[:, 8 : 8 + units // 128].reshape(depth, 8, 1, units)
+    bias = lax.dynamic_index_in_dim(bias, (place.x * 2 + place.c) * 2 + place.y, 1, keepdims=False)
+    width = tokens.shape[2]
+    W = G.reshape(PIECES, 2, width, -1)
+    length = tokens.shape[1] * 2
+    short = encoder.shape[1] * 2
+    tok = tok_row.reshape(length, width).astype(f32)
+    enc = enc_row.reshape(short, width)
+    up = lax.dynamic_index_in_dim(
+        g3.reshape(2, 2, 2, length, width)[place.x, place.c], place.y, 0, keepdims=False
+    )
+    target = lax.dynamic_index_in_dim(target_doc, place.y, 0, keepdims=False)
+    source = lax.dynamic_index_in_dim(source_doc, place.y, 0, keepdims=False)
+    positions = jnp.arange(length)
+    self_allowed = (target[:, None] == target[None, :]) & (positions[None, :] <= positions[:, None])
+    cross_allowed = target[:, None] == source[None, :]
+
+    def project(a, i):
+        return ein("td,ydj->tyj", a, W[i]).reshape(a.shape[0], width)
+
+    def project_back(a, i):
+        return ein("tyj,ydj->td", a.reshape(a.shape[0], 2, -1), W[i])
+
+    def weight_grad(a, b):
+        return ein("td,tyj->ydj", a, b.reshape(b.shape[0], 2, -1)).astype(bf)
+
+    n1, normal1, inverse1 = norm_forward(tok, sg, ss)
+    n1 = n1.astype(bf)
+    q, k, v = [project(n1, i).astype(bf) for i in range(3)]
+    heads1, lse1 = attend(q, k, v, self_allowed)
+    middle = tok + project_back(heads1, 3)
+    n2, normal2, inverse2 = norm_forward(middle, cg, cs)
+    n2 = n2.astype(bf)
+    cq = project(n2, 6).astype(bf)
+    ck, cv = project(enc, 4).astype(bf), project(enc, 5).astype(bf)
+    heads2, lse2 = attend(cq, ck, cv, cross_allowed)
+    latter = middle + project_back(heads2, 7)
+    n3, normal3, inverse3 = norm_forward(latter, hg, hs)
+    y, slope, gin, gout, gbias = hidden_block(n3.astype(bf), bias, win, wout, g3)
+    result = latter + y + ob
+    up = up.astype(f32)
+    g_ob = jnp.sum(up, axis=0)
+    slope, g_hg, g_hs = norm_backward(slope, normal3, inverse3, hg)
+    up = up + slope
+    low = up.astype(bf)
+    slope = project(low, 7).astype(bf)
+    dcq, dck, dcv = attend_backward(cq, ck, cv, cross_allowed, lse2, slope)
+    part_co = weight_grad(low, heads2)
+    part_cq = weight_grad(n2, dcq)
+    part_ck = weight_grad(enc, dck)
+    part_cv = weight_grad(enc, dcv)
+    enc_grad = project_back(dck, 4) + project_back(dcv, 5)
+    slope, g_cg, g_cs = norm_backward(project_back(dcq, 6), normal2, inverse2, cg)
+    up = up + slope
+    low = up.astype(bf)
+    slope = project(low, 3).astype(bf)
+    dq, dk, dv = attend_backward(q, k, v, self_allowed, lse1, slope)
+    part_so = weight_grad(low, heads1)
+    parts = [weight_grad(n1, d) for d in (dq, dk, dv)]
+    slope = project_back(dq, 0) + project_back(dk, 1) + project_back(dv, 2)
+    slope, g_sg, g_ss = norm_backward(slope, normal1, inverse1, sg)
+    tok_grad = up + slope
+    part = jnp.stack([part_co, part_cq, part_ck, part_cv, part_so] + parts).reshape(G.shape)
+    vg = jnp.stack([g_sg, g_ss, g_cg, g_cs, g_hg, g_hs, g_ob]).reshape(7, count, span).transpose(1, 0, 2)
+    vg = jnp.pad(vg, ((0, 0), (0, 1), (0, 128 - span)))
+    gw, vout, res, tg, eg = reduce_all(part, vg, result, tok_grad, enc_grad)
+    return (
+        res, tg, eg,
+        jnp.stack([gw[5], gw[6], gw[7]], axis=1),
+        gw[4].T, gw[1], jnp.stack([gw[2], gw[3]], axis=1), gw[0].T,
+        gin.T, gbias[0], gout,
+        vout[6, :span], vout[0, :span], vout[1, :span], vout[2, :span], vout[3, :span], vout[4, :span], vout[5, :span],
+    )
+
+
 BLOCK_ROWS = 512
 
 
@@ -15,14 +982,14 @@
     return jax.nn.gelu(values, approximate=True)
 
 
-def norm_forward(hidden, norm_gain, norm_shift):
+def plain_norm_forward(hidden, norm_gain, norm_shift):
     center = hidden - jnp.mean(hidden, axis=-1, keepdims=True)
     inverse = lax.rsqrt(jnp.mean(center * center, axis=-1, keepdims=True) + EPS)
     normal = center * inverse
     return (normal * norm_gain + norm_shift, normal, inverse)
 
 
-def norm_backward(upward, normal, inverse, norm_gain):
+def plain_norm_backward(upward, normal, inverse, norm_gain):
     scaled = upward * norm_gain
     centred = (
         scaled
@@ -47,7 +1014,7 @@
     return jnp.where(allow_block[None], scores, NEGATIVE)
 
 
-def attend(queries, key_rows, values, allowed):
+def plain_attend(queries, key_rows, values, allowed):
     columns = queries.shape[1]
     value_heads = values.reshape(values.shape[0], -1, HEAD)
 
@@ -70,7 +1037,7 @@
     return (mixture.reshape(queries.shape), logsum)
 
 
-def attend_backward(queries, key_rows, values, allowed, logsum, slope_heads):
+def plain_attend_backward(queries, key_rows, values, allowed, logsum, slope_heads):
     scaling = HEAD ** (-0.5)
     key_heads = key_rows.reshape(key_rows.shape[0], -1, HEAD)
     value_heads = values.reshape(values.shape[0], -1, HEAD)
@@ -155,7 +1122,7 @@
     )
 
 
-def local(
+def plain_local(
     tokens,
     encoder,
     target_doc,
@@ -230,18 +1197,18 @@
         )
         cross_allowed = target_row[:, None] == source_row[None, :]
         start_hidden = tokens[step_index].astype(jnp.float32)
-        normed_first, normal_first, inverse_first = norm_forward(
+        normed_first, normal_first, inverse_first = plain_norm_forward(
             start_hidden, full_self_gain, full_self_shift
         )
         self_rows = gather_rows(normed_first.astype(jnp.bfloat16))
         triple = jnp.einsum(
             "td,dcj->tcj", self_rows, full_proj, preferred_element_type=jnp.float32
         ).astype(jnp.bfloat16)
-        self_heads, self_logsum = attend(triple[:, 0], triple[:, 1], triple[:, 2], self_allowed)
+        self_heads, self_logsum = plain_attend(triple[:, 0], triple[:, 1], triple[:, 2], self_allowed)
         middle = start_hidden + sum_rows(
             jnp.dot(self_heads, full_self_out, preferred_element_type=jnp.float32)
         )
-        normed_second, normal_second, inverse_second = norm_forward(
+        normed_second, normal_second, inverse_second = plain_norm_forward(
             middle, full_cross_gain, full_cross_shift
         )
         cross_rows, source_rows = (
@@ -254,13 +1221,13 @@
         key_value = jnp.einsum(
             "sd,dcj->scj", source_rows, full_pairs, preferred_element_type=jnp.float32
         ).astype(jnp.bfloat16)
-        cross_heads, cross_logsum = attend(
+        cross_heads, cross_logsum = plain_attend(
             cross_queries, key_value[:, 0], key_value[:, 1], cross_allowed
         )
         latter = middle + sum_rows(
             jnp.dot(cross_heads, full_cross_out, preferred_element_type=jnp.float32)
         )
-        normed_third, normal_third, inverse_third = norm_forward(
+        normed_third, normal_third, inverse_third = plain_norm_forward(
             latter, full_hidden_gain, full_hidden_shift
         )
         hidden_rows = gather_rows(normed_third.astype(jnp.bfloat16))
@@ -309,7 +1276,7 @@
         slope_normed = sum_slopes(
             jnp.einsum("tf,df->td", slope_before, back_in, preferred_element_type=jnp.float32)
         )
-        slope_hidden, grad_hidden_gain, grad_hidden_shift = norm_backward(
+        slope_hidden, grad_hidden_gain, grad_hidden_shift = plain_norm_backward(
             slope_normed, normal_third, inverse_third, full_hidden_gain
         )
         upward = upward + slope_hidden
@@ -320,7 +1287,7 @@
         slope_heads = jnp.einsum(
             "td,jd->tj", slope_rows, back_cross_out, preferred_element_type=jnp.float32
         ).astype(jnp.bfloat16)
-        slope_query, slope_keys, slope_values = attend_backward(
+        slope_query, slope_keys, slope_values = plain_attend_backward(
             cross_queries,
             key_value[:, 0],
             key_value[:, 1],
@@ -353,7 +1320,7 @@
                 tiled=True,
             ).astype(jnp.float32),
         )
-        slope_hidden, grad_cross_gain, grad_cross_shift = norm_backward(
+        slope_hidden, grad_cross_gain, grad_cross_shift = plain_norm_backward(
             slope_cross, normal_second, inverse_second, full_cross_gain
         )
         upward = upward + slope_hidden
@@ -364,7 +1331,7 @@
         slope_heads = jnp.einsum(
             "td,jd->tj", slope_rows, back_self_out, preferred_element_type=jnp.float32
         ).astype(jnp.bfloat16)
-        slope_query, slope_keys, slope_values = attend_backward(
+        slope_query, slope_keys, slope_values = plain_attend_backward(
             triple[:, 0], triple[:, 1], triple[:, 2], self_allowed, self_logsum, slope_heads
         )
         slope_triple = jnp.stack([slope_query, slope_keys, slope_values], axis=1)
@@ -374,7 +1341,7 @@
         slope_self = sum_slopes(
             jnp.einsum("tcj,dcj->td", slope_triple, back_proj, preferred_element_type=jnp.float32)
         )
-        slope_hidden, grad_self_gain, grad_self_shift = norm_backward(
+        slope_hidden, grad_self_gain, grad_self_shift = plain_norm_backward(
             slope_self, normal_first, inverse_first, full_self_gain
         )
         token_grads.append(upward + slope_hidden)
@@ -479,4 +1446,11 @@
         P(("dp", "tensor")),
         P(("dp", "tensor")),
     )
-    return jax.shard_map(local, mesh=mesh, in_specs=in_specs, out_specs=out_specs, check_vma=False)
+
+    def run(*arrays):
+        width = arrays[0].shape[2]
+        aligned = width // mesh.shape["dp"] % 16 == 0 and mesh.shape["dp"] % 4 == 0
+        inner = fast_local if aligned and mesh.shape["tensor"] == 2 else plain_local
+        return jax.shard_map(inner, mesh=mesh, in_specs=in_specs, out_specs=out_specs, check_vma=False)(*arrays)
+
+    return run

time: 1440 us -> 633 us (0.44)
  waiting for transfers between devices: 834 us -> 0 us
  Pallas kernels: 0 us -> 409 us
  blocking collectives: 272 us -> 0 us
  matrix products: 185 us -> 59.4 us
  local copies, waits for them, and re-layouts: 71 us -> 140 us
  other arithmetic: 42.9 us -> 12 us
  between operations: 17.9 us -> 2.04 us
    reduce_scatter x20 -> x0, waiting for transfers between devices: 636 us -> none  [the longest x1 183 us: reduce_weights(): lax.psum_scatter(weight_terms[7], 'dp', scatter_dimension=0, tiled=True)]
    pallas_call x0 -> x3, Pallas kernels: none -> 409 us  [the longest x1 169 us: hidden_block(): pl.pallas_call(functools.partial(hidden_kernel, depth), out_shape=[jax.Sh...]
    all_gather x7 -> x0, waiting for transfers between devices: 194 us -> none  [the longest x1 67.5 us: local(): lax.all_gather(hidden_out, 'dp', axis=0, tiled=True)]
    unnamed x3 -> x0, blocking collectives: 140 us -> none
    all_gather x15 -> x0, blocking collectives: 132 us -> none  [the longest x6 50 us: gather_slopes(): return lax.all_gather(local_slopes, 'tensor', axis=0, tiled=True)]
    dot_general x66 -> x36, matrix products: 185 us -> 59.4 us  [ein(): return jnp.einsum(form, *operands, preferred_element_type=jnp.float32)]
    dot_general x0 -> x8, local copies, waits for them, and re-layouts: none -> 23.4 us  [ein(): return jnp.einsum(form, *operands, preferred_element_type=jnp.float32)]
    convert_element_type x16, local copies, waits for them, and re-layouts: 21.1 us -> 42.5 us  [the longest x8 31 us: weight_grad(): return ein('td,tyj->ydj', a, b.reshape(b.shape[0], 2, -1)).astype(bf)]
  transfers between devices with their start and end apart: 28 -> 0, of which waited for: 15 -> 0; matrix products, arithmetic and copies ran while one was open for 17% -> 0% of each run, Pallas kernels for 0% -> 0%
where the time goes in v1:
time: 633 us; the launch traced here: 623 us
  Pallas kernels  409 us (65%)
  local copies, waits for them, and re-layouts  140 us (22%)
  matrix products  59.4 us (9%)
  other arithmetic  12 us (2%)
    pallas_call x1, Pallas kernels, hidden_block(): pl.pallas_call(functools.partial(hidden_kernel, depth), out_shape=[jax.Sh...  169 us
    pallas_call x1, Pallas kernels, gather_all(): pl.pallas_call(functools.partial(gather_kernel, depth), out_shape=out_sha...  135 us
    pallas_call x1, Pallas kernels, reduce_all(): pl.pallas_call(functools.partial(reduce_kernel, depth), out_shape=[jax.Sh...  106 us
    dot_general x36, matrix products, ein(): return jnp.einsum(form, *operands, preferred_element_type=jnp.float32)  59.4 us
    unnamed x184, local copies, waits for them, and re-layouts  47.8 us
    convert_element_type x8, local copies, waits for them, and re-layouts, weight_grad(): return ein('td,tyj->ydj', a, b.reshape(b.shape[0], 2, -1)).astype(bf)  31 us
    dot_general x8, local copies, waits for them, and re-layouts, ein(): return jnp.einsum(form, *operands, preferred_element_type=jnp.float32)  23.4 us
    slice x1, local copies, waits for them, and re-layouts, project_back(): return ein('tyj,ydj->td', a.reshape(a.shape[0], 2, -1), W[i])  14.3 us

profile of v1, /device:TPU:0, one launch (start us, length us, event | category | flops | bytes accessed | tf_op | source)
XLA Modules:
  0.0 622.8 jit_solution(7677395843197656936)
XLA Ops:
  10.9 135.0 %gather_all.1 = (bf16[8,2,4,2,2,64,512]{6,5,4,3,2,1,0:T(8,128)(2,1)S(1)}, bf16[4,1024,256]{2,1,0:T(8,128)(2,1)S(1)}, bf16[4,256,1024]{2,1,0:T(8,128)(2,1)S(1)}, ...) custom-call(bf16[8,64,512]{2,1,0:T(8,128)(2,1)S(1)} %bitcast_dynamic, ...), custom_call_target="tpu_custom_call" | custom-call | tf_op jit(solution)/shard_map/gather_all/pallas_call | solution.py:311
  145.9 5.7 copy-done.2
  151.6 1.3 copy-done.4
  152.9 14.3 %fusion.39 = (bf16[1,2,4,2,2,64,512]{6,5,4,3,2,1,0:T(8,128)(2,1)}, bf16[1,2,4,2,2,64,512]{6,5,4,3,2,1,0:T(8,128)(2,1)}, bf16[1,2,4,2,2,64,512]{6,5,4,3,2,1,0:T(8...) fusion(bf16[8,2,4,2,2,64,512]{6,5,4,3,2,1,0:T(8,128)(2,1)} %cop, ...), kind=kLoop, calls=%fused_computation.161 | loop fusion | bytes 33554432 | tf_op jit(solution)/shard_map/slice | solution.py:924
  169.5 4.2 copy.85
  173.6 3.3 convolution_convert_fusion.9
  176.9 1.8 copy.86
  178.7 2.5 copy.87
  181.2 3.3 convolution_convert_fusion.6
  184.5 2.0 copy.88
  186.5 2.5 copy.89
  189.0 3.3 convolution_convert_fusion.5
  192.3 2.1 copy.90
  194.4 2.5 copy.91
  196.9 3.3 convolution_convert_fusion.4
  200.1 2.0 copy.92
  202.2 2.5 copy.113
  204.6 4.1 copy.95
  208.8 2.5 copy.97
  211.3 2.6 convolution_convert_fusion.8
  214.7 2.7 copy.103
  217.4 1.9 fusion.42
  219.9 1.3 copy-done.11
  230.5 168.6 %hidden_block.1 = (f32[256,1024]{1,0:T(8,128)}, f32[256,1024]{1,0:T(8,128)}, f32[256,1024]{1,0:T(8,128)}, f32[256,1024]{1,0:T(8,128)}, f32[8,256]{1,0:T(8,128)}) custom-call(bf16[256,1024]{1,0:T(8,128)(2,1)} %add_convert_fusion.hn_ref, f32[4,1,256]{2,1,0:T(1,128)} %dynamic-slice_bitcast_fusion.bias_ref, bf16[4,1024,256]{2,1,0:T(8,128)(2,1)} %copy-done.4, ...), custom_call_target="tpu_custom_call" | custom-call | tf_op jit(solution)/shard_map/hidden_block/pallas_call | solution.py:612
  399.1 2.6 copy.127
  401.8 1.3 slice.167
  403.6 2.6 add_add_fusion
  407.2 1.6 convolution_convert_fusion.2
  408.7 1.2 copy.104
  418.2 1.6 fusion.19.eg_ref
  421.4 1.6 convolution_convert_fusion.1
  423.0 1.2 copy.114
  424.4 3.2 convert_bitcast_fusion.6
  427.7 3.9 copy.106
  431.6 3.1 fusion.12
  434.7 1.7 convolution_bitcast_fusion
  436.5 2.1 convert_bitcast_fusion.7
  438.6 4.0 copy.102
  442.6 2.1 convert_bitcast_fusion
  444.7 4.1 copy.120
  448.8 2.1 convert_bitcast_fusion.3
  450.9 4.0 copy.112
  454.9 2.1 convert_bitcast_fusion.5
  457.0 4.0 copy.108
  461.0 2.1 convert_bitcast_fusion.4
  463.1 4.0 copy.110
  467.1 3.4 multiply_reduce_fusion
  473.2 1.4 copy-done.20
  476.7 1.4 multiply_add_fusion.tg_ref
  479.1 1.8 convert_bitcast_fusion.2
  480.9 2.6 copy.116
  483.5 2.0 convert_bitcast_fusion.1
  485.6 4.3 copy.118
  489.9 1.5 constant_dynamic-update-slice_fusion.7
  492.3 1.5 constant_dynamic-update-slice_fusion.6
  494.6 1.6 constant_dynamic-update-slice_fusion.5
  497.0 1.6 constant_dynamic-update-slice_fusion.4
  499.3 1.6 constant_dynamic-update-slice_fusion.3
  501.7 1.6 constant_dynamic-update-slice_fusion.2
  504.0 1.5 constant_dynamic-update-slice_fusion.1
  506.4 1.5 constant_dynamic-update-slice_fusion.part
  507.9 105.5 %reduce_all.1 = (f32[8,64,512]{2,1,0:T(8,128)}, f32[8,128]{1,0:T(8,128)}, f32[2,128,1024]{2,1,0:T(8,128)}, f32[2,128,1024]{2,1,0:T(8,128)}, f32[2,64,1024]{2,1,0:T(8,128)}) custom-call(bf16[8,2,4,2,2,64,512]{6,5,4,3,2,1,0:T(8,128)(2,1)} %constant_dynamic-update-slice_fusion.part, f32[32,8,128]{2,1,0:T(8,128)} %pad.9.vec_ref, ...), custom_call_target="tpu_custom_call" | custom-call | tf_op jit(solution)/shard_map/reduce_all/pallas_call | solution.py:784
  613.4 1.5 slice_bitcast_fusion.8
  614.9 2.1 slice_bitcast_fusion
  (247 shorter events, 50.7 us)
Async XLA Ops:
  0.7 9.1 %copy-start.7 = (bf16[256,1024]{1,0:T(8,128)(2,1)S(1)}, bf16[256,1024]{1,0:T(8,128)(2,1)}, u32[]{:S(2)}) copy-start(bf16[256,1024]{1,0:T(8,128)(2,1)} %wout_ref.1) | copy-start | bytes 1572868
  0.7 9.1 %copy-start.6 = (bf16[1024,256]{1,0:T(8,128)(2,1)S(1)}, bf16[1024,256]{1,0:T(8,128)(2,1)}, u32[]{:S(2)}) copy-start(bf16[1024,256]{1,0:T(8,128)(2,1)} %win_ref.1) | copy-start | bytes 1572868
  0.7 9.1 %copy-start.10 = (bf16[2,64,1024]{2,1,0:T(8,128)(2,1)S(1)}, bf16[2,64,1024]{2,1,0:T(8,128)(2,1)}, u32[]{:S(2)}) copy-start(bf16[2,64,1024]{2,1,0:T(8,128)(2,1)} %enc_ref.1) | copy-start | bytes 786436
  0.7 9.1 %copy-start.8 = (bf16[2,128,1024]{2,1,0:T(8,128)(2,1)S(1)}, bf16[2,128,1024]{2,1,0:T(8,128)(2,1)}, u32[]{:S(2)}) copy-start(bf16[2,128,1024]{2,1,0:T(8,128)(2,1)} %tok_ref.1) | copy-start | bytes 1572868
  145.9 5.7 copy-start.2
  152.9 14.3 %copy-start.5 = (bf16[4,256,1024]{2,1,0:T(8,128)(2,1)}, bf16[4,256,1024]{2,1,0:T(8,128)(2,1)S(1)}, u32[]{:S(2)}) copy-start(bf16[4,256,1024]{2,1,0:T(8,128)(2,1)S(1)} %get-tuple-element.41.Wout) | copy-start | bytes 6291460
  152.9 15.4 %copy-start.3 = (bf16[2,2,2,2,128,1024]{5,4,3,2,1,0:T(8,128)(2,1)}, bf16[2,2,2,2,128,1024]{5,4,3,2,1,0:T(8,128)(2,1)S(1)}, u32[]{:S(2)}) copy-start(bf16[2,2,2,2,128,1024]{5,4,3,2,1,0:T(8,128)(2,1)S(1)} %get-tuple-element.39.g3) | copy-start | bytes 12582916
  169.5 27.4 %copy-start.44 = (bf16[2,128,1024]{2,1,0:T(8,128)(2,1)}, bf16[2,128,1024]{2,1,0:T(8,128)(2,1)S(1)}, u32[]{:S(2)}) copy-start(bf16[2,128,1024]{2,1,0:T(8,128)(2,1)S(1)} %add_convert_fusion.2) | copy-start | bytes 1572868
  173.6 5.1 copy-start.21
  181.2 5.3 copy-start.17
  189.0 5.3 copy-start.19
  196.8 5.3 copy-start.28
  204.6 4.1 copy-start.23
  211.3 3.4 copy-start.26
  214.7 2.7 copy-start.53
  219.3 1.9 copy-start.11
  219.3 1.9 copy-start.69
  221.3 1.6 copy-start.29
  223.7 3.7 copy-start.15
  226.6 1.7 copy-start.27
  227.4 1.8 copy-start.66
  399.1 4.0 copy-start.57
  401.8 1.9 copy-start.77
  403.6 3.5 copy-start.35
  407.2 3.0 copy-start.14
  410.2 1.7 copy-start.25
  410.7 2.6 copy-start.62
  410.7 2.0 copy-start.73
  414.4 2.2 copy-start.33
  414.4 2.2 copy-start.81
  414.9 2.8 copy-start.60
  415.2 2.5 copy-start.68
  417.6 2.2 copy-start.31
  424.2 7.4 %copy-start.46 = (bf16[256,1024]{0,1:T(8,128)(2,1)}, bf16[256,1024]{0,1:T(8,128)(2,1)S(1)}, u32[]{:S(2)}) copy-start(bf16[256,1024]{0,1:T(8,128)(2,1)S(1)} %copy.114) | copy-start | bytes 1572868
  431.6 3.1 copy-start.22
  434.7 1.8 copy-start.32
  434.7 1.8 copy-start.67
  438.6 4.0 copy-start.45
  444.7 4.1 copy-start.65
  450.9 4.0 copy-start.61
  457.0 4.0 copy-start.63
  463.1 4.0 copy-start.47
  463.1 4.0 copy-start.70
  467.1 3.5 copy-start.12
  472.6 2.7 copy-start.50
  472.6 2.0 copy-start.20
  473.1 3.6 copy-start.52
  473.1 2.2 copy-start.18
  473.1 2.4 copy-start.56
  473.2 2.4 copy-start.79
  480.9 2.6 copy-start.51
  485.6 4.4 copy-start.39
  489.9 2.3 copy-start.37
  492.3 2.3 copy-start.40
  494.6 2.3 copy-start.41
  497.0 2.3 copy-start.38
  499.3 2.3 copy-start.42
  501.7 2.3 copy-start.43
  504.0 2.3 copy-start.36
  613.4 5.3 copy-start.76
  617.0 2.7 copy-start.75
  618.7 2.0 copy-start.78
  619.7 1.8 copy-start.74
  619.7 2.7 copy-start.1
  (18 other events, 21.8 us)
